TPU v7x, 512 devices: a whole 4x4x16 slice. The times are simulated.
512 devices in a mesh: req: 16 (over y, z_hi), head: 32 (over z_lo, x, core).
Axes of the slice: x: 4, y: 4, z: 16 (z_hi: 4, z_lo: 4; z = z_hi * 4 + z_lo), core: 2. Of those that a mesh axis runs over, the one named last changes fastest.
Arguments:
- queries: bfloat16 [6144, 128, 192], P('req', 'head'), may hold values from -128 to 128
- d_out: bfloat16 [6144, 128, 128], P('req', 'head'), may hold values from -6 to 6
- tok_latent: bfloat16 [6144, 576], P('req'), may hold values from -6 to 6
- w_uk: bfloat16 [128, 128, 512], P('head'), may hold values from -0.5 to 0.5
- w_uv: bfloat16 [128, 512, 128], P('head'), may hold values from -0.25 to 0.25
- pool: float32 [16, 64, 576], P('req', 'head'), may hold values from -6 to 6
- tenant_of_request: int32 [16], replicated, may hold values from 0 to 15
- slot_of_tenant: int32 [16], replicated, may hold values from 0 to 15, each once
Outputs:
- d_queries: bfloat16 [6144, 128, 192], P('req', 'head')
- d_tok_latent: bfloat16 [6144, 576], P(('req', 'head'))
- pool_grad: float32 [16, 64, 576], P('req', 'head')
All inputs are finite; a program needn't handle non-finite values.
Results may differ from a plain program's by a relative error of at most 0.035.
Values may be sent and summed in bfloat16 or wider, within the bound.
No kernel may reach another device: no remote copies, remote signals or barrier semaphores. Data moves between devices by JAX's collectives and lax.ppermute only.
A program may use at most 64 MiB of HBM per device.

v0:
```python
import jax
import jax.numpy as jnp
from jax import lax
from jax.sharding import PartitionSpec as P

D_LAT = 512
D_ROPE = 64
D_NOPE = 128


def shards(queries, d_out, tok_latent, w_uk, w_uv, pool, tenant_of_request, slot_of_tenant):
    score_scale = float(D_NOPE + D_ROPE) ** (-0.5)
    req_place = lax.axis_index("req")
    slot_ids = slot_of_tenant[tenant_of_request]
    my_slot = lax.dynamic_index_in_dim(slot_ids, req_place, 0, keepdims=False)
    pool_half = pool.astype(jnp.bfloat16)
    slots_dev = pool.shape[0]
    head_count = lax.axis_size("head")
    group_rows = lax.all_gather(pool_half, "head", axis=1, tiled=True)
    shard_piece = lax.all_gather(group_rows, "req", axis=0, tiled=True)
    numbers = jnp.arange(shard_piece.shape[0], dtype=jnp.int32)
    chosen = jnp.where((numbers == my_slot)[:, None, None], shard_piece.astype(jnp.float32), 0.0)
    fetched = jnp.sum(chosen, axis=0)
    prefix = fetched.astype(jnp.bfloat16)
    prefix_rows = prefix.shape[0]
    seq_len = queries.shape[0]
    all_keys = jnp.concatenate([prefix, tok_latent], axis=0)
    values = all_keys[:, :D_LAT]
    query_lat = jnp.einsum(
        "shn,hnl->hsl", queries[:, :, :D_NOPE], w_uk, preferred_element_type=jnp.float32
    ).astype(jnp.bfloat16)
    query_rope = jnp.transpose(queries[:, :, D_NOPE:], (1, 0, 2))
    query_full = jnp.concatenate([query_lat, query_rope], axis=2)
    scores = (
        jnp.einsum("hsl,kl->hsk", query_full, all_keys, preferred_element_type=jnp.float32)
        * score_scale
    )
    row_pos = jnp.arange(seq_len, dtype=jnp.int32)[:, None]
    col_pos = jnp.arange(all_keys.shape[0], dtype=jnp.int32)[None, :]
    visible = ((col_pos < prefix_rows) | (col_pos - prefix_rows <= row_pos))[None]
    scores = jnp.where(visible, scores, -1e30)
    row_top = jnp.max(scores, axis=2, keepdims=True)
    exp_terms = jnp.where(visible, jnp.exp(scores - row_top), 0.0)
    attn_probs = exp_terms / jnp.sum(exp_terms, axis=2, keepdims=True)
    probs_half = attn_probs.astype(jnp.bfloat16)
    out_lat = jnp.einsum("hsk,kl->hsl", probs_half, values, preferred_element_type=jnp.float32)
    dout_lat = jnp.einsum("shv,hlv->hsl", d_out, w_uv, preferred_element_type=jnp.float32).astype(
        jnp.bfloat16
    )
    d_probs = jnp.einsum("hsl,kl->hsk", dout_lat, values, preferred_element_type=jnp.float32)
    delta_row = jnp.sum(dout_lat.astype(jnp.float32) * out_lat, axis=2, keepdims=True)
    d_scores = (attn_probs * (d_probs - delta_row) * score_scale).astype(jnp.bfloat16)
    d_query = jnp.einsum("hsk,kl->hsl", d_scores, all_keys, preferred_element_type=jnp.float32)
    d_nope = jnp.einsum(
        "hsl,hnl->shn",
        d_query[:, :, :D_LAT].astype(jnp.bfloat16),
        w_uk,
        preferred_element_type=jnp.float32,
    )
    d_rope = jnp.transpose(d_query[:, :, D_LAT:], (1, 0, 2))
    d_queries = jnp.concatenate([d_nope, d_rope], axis=2).astype(jnp.bfloat16)

    def key_block(first_row, row_count):
        score_part = lax.dynamic_slice_in_dim(d_scores, first_row, row_count, 2)
        probs_part = lax.dynamic_slice_in_dim(probs_half, first_row, row_count, 2)
        key_grad = jnp.einsum(
            "hsk,hsl->kl", score_part, query_full, preferred_element_type=jnp.float32
        )
        value_grad = jnp.einsum(
            "hsk,hsl->kl", probs_part, dout_lat, preferred_element_type=jnp.float32
        )
        return jnp.concatenate([key_grad[:, :D_LAT] + value_grad, key_grad[:, D_LAT:]], axis=1)

    token_dev = seq_len // head_count
    token_grad = lax.psum_scatter(
        key_block(prefix_rows + jnp.int32(0), token_dev * lax.axis_size("head")).astype(
            jnp.bfloat16
        ),
        "head",
        scatter_dimension=0,
        tiled=True,
    )
    prefix_grad = key_block(0, prefix_rows)
    share_grad = lax.psum_scatter(
        prefix_grad.astype(jnp.bfloat16), "head", scatter_dimension=0, tiled=True
    ).astype(jnp.float32)
    req_count = lax.axis_size("req")
    owned_slot = (jnp.arange(req_count * slots_dev, dtype=jnp.int32) == my_slot)[:, None, None]
    placed = jnp.where(owned_slot, share_grad[None], 0.0)
    pool_grad = lax.psum_scatter(
        placed.astype(jnp.bfloat16), "req", scatter_dimension=0, tiled=True
    ).astype(jnp.float32)
    return (d_queries, token_grad, pool_grad)


def solution(mesh):
    return jax.shard_map(
        shards,
        mesh=mesh,
        in_specs=(
            P("req", "head", None),
            P("req", "head", None),
            P("req", None),
            P("head", None, None),
            P("head", None, None),
            P("req", "head", None),
            P(),
            P(),
        ),
        out_specs=(P("req", "head", None), P(("req", "head"), None), P("req", "head", None)),
        check_vma=False,
    )
```

profile of v0, /device:TPU:6, one launch (start us, length us, event | category | flops | bytes accessed | tf_op | source)
XLA Modules:
  0.0 532.3 jit_solution(14823024320441379218)
XLA Ops:
  7.2 0.0 copy-start
  7.2 0.0 slice-start
  7.2 0.0 all-gather.2.cloned.1.call-start
  7.3 0.8 copy.60
  8.1 39.3 %all_gather.6 = bf16[1,64,576]{2,0,1:T(2,128)(2,1)S(1)} all-gather(bf16[1,2,576]{2,0,1:T(2,128)(2,1)S(1)} %copy.60), channel_id=1, replica_groups=mesh['req'=16,'head'=32] {'head'}, dimensions={1}, use_global_device_ids=true | all-gather | bytes 76032 | tf_op jit(solution)/shard_map/all_gather | solution.py:19
  47.3 0.6 copy.36
  48.0 0.0 all-gather.2.cloned.1.call-update
  48.0 0.0 all-reduce.6.cloned.1.call-start
  48.1 1.3 copy.37
  49.3 0.0 copy-start.5
  49.4 0.0 copy-start.6
  49.4 0.9 copy.56
  50.3 1.3 dynamic-slice
  52.9 1.3 dynamic-slice.4
  54.2 0.0 copy-done.1
  54.2 0.7 gather_fusion
  54.9 0.6 dynamic_slice.16
  55.5 0.6 iota_compare_fusion.2
  56.1 0.9 fusion.20
  57.0 1.8 convolution_convert_fusion.2
  58.8 0.6 convolution_convert_fusion.1
  59.4 75.7 %all-gather.2.cloned.1.call-done = bf16[16,64,576]{2,1,0:T(8,128)(2,1)} async-done(((bf16[1,64,576]{2,1,0:T(8,128)(2,1)}), bf16[16,64,576]{2,1,0:T(8,128)(2,1)}) %all-gather.2.cloned.1.call-update) | async-done | bytes 1179664 | tf_op jit(solution)/shard_map/all_gather | solution.py:20
  135.0 1.7 select_reduce_fusion
  136.7 5.1 fusion.41
  141.8 2.0 fusion.19
  143.8 1.1 multiply_reduce_fusion
  144.9 0.6 copy-done.2
  145.6 1.0 multiply_convert_fusion
  146.6 0.4 copy-done.3
  147.0 0.1 copy-done.7
  147.0 0.5 convolution_bitcast_fusion.2
  147.5 0.4 fusion.18
  147.9 1.1 convolution_bitcast_fusion
  149.1 1.0 fusion.8
  150.1 2.4 convolution_convert_fusion
  152.5 0.6 pad_maximum_fusion.7
  153.1 0.8 pad_maximum_fusion.6
  153.9 0.0 all-reduce.6.cloned.1.call-update
  154.0 1.0 slice_bitcast_fusion
  154.9 1.9 fusion.12
  156.8 0.9 pad_maximum_fusion.2
  157.7 266.8 %all-reduce.6.cloned.1.call-done = (bf16[384,576]{0,1:T(8,128)(2,1)}, bf16[64,576]{1,0:T(8,128)(2,1)}) async-done(((bf16[384,576]{0,1:T(8,128)(2,1)}, bf16[64,576]{1,0:T(8,128)(2,1)}), (bf16[384,576]{0,1:T(8,128)(2,1)}, bf16[64,576]{1,0:T(8,128)(2,1)})) %all-reduce.6.cloned.1.call-update) | async-done | bytes 516112
  424.4 1.1 constant_dynamic-slice_fusion
  425.5 0.7 copy.45
  426.2 0.7 dynamic-slice_convert_fusion.1
  427.0 0.1 select_convert_fusion
  427.1 97.1 %all-reduce.2 = bf16[16,2,576]{2,1,0:T(2,128)(2,1)S(1)} all-reduce(bf16[16,2,576]{2,1,0:T(2,128)(2,1)S(1)} %select_convert_fusion), channel_id=4, replica_groups=mesh['req'=16,'head'=32] {'req'}, use_global_device_ids=true, to_apply=%region_6.7.clone | all-reduce | flops 18432 | bytes 73728
  524.2 1.3 dynamic-slice_convert_fusion
  (18 shorter events, 0.1 us)
Async XLA Ops:
  7.2 49.8 %copy-start = (bf16[4,128,512]{2,1,0:T(8,128)(2,1)S(1)}, bf16[4,128,512]{2,1,0:T(8,128)(2,1)}, u32[]{:S(2)}) copy-start(bf16[4,128,512]{2,1,0:T(8,128)(2,1)} %param.11) | copy-start | bytes 1572868
  7.2 42.2 %slice-start = ((bf16[384,4,192]{0,2,1:T(8,128)(2,1)}), bf16[384,4,64]{0,2,1:T(8,128)(2,1)S(1)}, s32[]{:S(2)}) async-start(bf16[384,4,192]{0,2,1:T(8,128)(2,1)} %param.8), calls=%async_computation.2 | async-start | bytes 393216 | tf_op jit(solution)/shard_map/slice | solution.py:32
  7.2 49.8 %copy-start.4 = (bf16[384,4,192]{0,2,1:T(8,128)(2,1)S(1)}, bf16[384,4,192]{0,2,1:T(8,128)(2,1)}, u32[]{:S(2)}) copy-start(bf16[384,4,192]{0,2,1:T(8,128)(2,1)} %param.8) | copy-start | bytes 1769476
  7.2 47.0 %copy-start.8 = (s32[16]{0:T(128)S(1)}, s32[16]{0:T(128)}, u32[]{:S(2)}) copy-start(s32[16]{0:T(128)} %param.14) | copy-start | bytes 196
  7.2 47.0 %copy-start.1 = (s32[16]{0:T(128)S(1)}, s32[16]{0:T(128)}, u32[]{:S(2)}) copy-start(s32[16]{0:T(128)} %param.15) | copy-start | bytes 196
  7.2 127.8 %all-gather.2.cloned.1.call-start = ((), (), s32[]{:S(2)}) async-start(), calls=%async_computation | async-start | bytes 1392640 | tf_op jit(solution)/shard_map/all_gather | solution.py:20
  48.0 376.4 %all-reduce.6.cloned.1.call-start = ((), (), s32[]{:S(2)}) async-start(), calls=%async_computation.1 | async-start | bytes 1048576
  49.3 9.4 %copy-start.5 = (bf16[4,512,128]{2,1,0:T(8,128)(2,1)S(1)}, bf16[4,512,128]{2,1,0:T(8,128)(2,1)}, u32[]{:S(2)}) copy-start(bf16[4,512,128]{2,1,0:T(8,128)(2,1)} %param.12) | copy-start | bytes 1572868
  49.4 9.4 %copy-start.6 = (bf16[384,4,128]{2,1,0:T(4,128)(2,1)S(1)}, bf16[384,4,128]{2,1,0:T(4,128)(2,1)}, u32[]{:S(2)}) copy-start(bf16[384,4,128]{2,1,0:T(4,128)(2,1)} %param.9) | copy-start | bytes 1179652
  143.8 1.8 copy-start.2
  145.6 1.4 copy-start.3
  145.6 1.5 copy-start.7
Sparse Core Ops, SparseCore 0:
  48.1 86.8 all-gather.1
  154.1 270.2 all-reduce.5
where the time goes:
time: 541 us; the launch traced here: 532 us
  waiting for transfers between devices  342 us (63%)
  blocking collectives  136 us (25%)
  matrix products  16.8 us (3%)
  between operations  15.5 us (3%)
  local copies, waits for them, and re-layouts  12.1 us (2%)
  other arithmetic  8.88 us (2%)
    unnamed x3, waiting for transfers between devices  267 us
    unnamed x1, blocking collectives  97.1 us
    all_gather x1, waiting for transfers between devices, shards(): shard_piece = lax.all_gather(group_rows, 'req', axis=0, tiled=True)  75.7 us
    all_gather x1, blocking collectives, shards(): group_rows = lax.all_gather(pool_half, 'head', axis=1, tiled=True)  39.3 us
  transfers between devices with their start and end apart: 2, of which 2 were waited for; matrix products, arithmetic and copies ran while one was open for 3% of the time, Pallas kernels for 0%

commit v1 on v0

v1 whole, which is shorter than its diff:
```python
import jax
import jax.numpy as jnp
from jax import lax
from jax.sharding import PartitionSpec as P

D_LAT = 512
D_ROPE = 64
D_NOPE = 128
CHUNK = 16
bf16 = jnp.bfloat16
f32 = jnp.float32


def shards(queries, d_out, tok_latent, w_uk, w_uv, pool, tenant_of_request, slot_of_tenant):
    score_scale = float(D_NOPE + D_ROPE) ** (-0.5)
    heads = lax.axis_size("head")
    reqs = lax.axis_size("req")
    req_place = lax.axis_index("req")
    slot_ids = slot_of_tenant[tenant_of_request]
    my_slot = lax.dynamic_index_in_dim(slot_ids, req_place, 0, keepdims=False)
    lat = pool.shape[2]
    pre = pool.shape[1]
    seq = queries.shape[0]
    tok = seq // heads

    with jax.named_scope("fetch_slots"):
        mine = jnp.broadcast_to(pool.astype(bf16), (reqs, pre, lat))
        all_slots = lax.all_to_all(mine, "req", 0, 0)
    with jax.named_scope("spread_prefix"):
        rows = lax.dynamic_index_in_dim(all_slots, my_slot, 0, keepdims=True)
        prefix = lax.all_to_all(jnp.broadcast_to(rows, (heads, pre, lat)), "head", 0, 0)

    with jax.named_scope("keys"):
        tokens = tok_latent.reshape(heads, tok, lat)
        spare = jnp.zeros((heads, CHUNK - pre - tok, lat), bf16)
        keys = jnp.concatenate([prefix, tokens, spare], axis=1).reshape(heads * CHUNK, lat)
        latents = keys[:, :D_LAT]
    key_h = jnp.einsum("kl,hnl->hkn", latents, w_uk, preferred_element_type=f32).astype(bf16)
    val_h = jnp.einsum("kl,hlv->hkv", latents, w_uv, preferred_element_type=f32).astype(bf16)
    q = jnp.transpose(queries, (1, 0, 2))
    do = jnp.transpose(d_out, (1, 0, 2))
    n_h = q.shape[0]
    rope = jnp.broadcast_to(keys[None, :, D_LAT:], (n_h, heads * CHUNK, D_ROPE))
    key_full = jnp.concatenate([key_h, rope], axis=2)
    scores = jnp.einsum("hsn,hkn->hsk", q, key_full, preferred_element_type=f32) * score_scale
    place = jnp.arange(heads * CHUNK, dtype=jnp.int32)
    chunk, inner = place // CHUNK, place % CHUNK
    number = chunk * tok + inner - pre
    earliest = jnp.where(inner < pre, 0, jnp.where(inner < pre + tok, number, seq))
    visible = (earliest[None, :] <= jnp.arange(seq, dtype=jnp.int32)[:, None])[None]
    scores = jnp.where(visible, scores, -1e30)
    top = jnp.max(scores, axis=2, keepdims=True)
    terms = jnp.where(visible, jnp.exp(scores - top), 0.0)
    probs = terms / jnp.sum(terms, axis=2, keepdims=True)
    probs_half = probs.astype(bf16)
    d_probs = jnp.einsum("hsv,hkv->hsk", do, val_h, preferred_element_type=f32)
    delta = jnp.sum(probs * d_probs, axis=2, keepdims=True)
    d_scores = (probs * (d_probs - delta) * score_scale).astype(bf16)
    d_queries = jnp.einsum("hsk,hkn->shn", d_scores, key_full, preferred_element_type=f32).astype(bf16)
    ds_q = jnp.einsum("hsk,hsn->hkn", d_scores, q, preferred_element_type=f32)
    p_do = jnp.einsum("hsk,hsv->hkv", probs_half, do, preferred_element_type=f32).astype(bf16)
    lat_grad = jnp.einsum("hkn,hnl->kl", ds_q[:, :, :D_NOPE].astype(bf16), w_uk, preferred_element_type=f32)
    lat_grad += jnp.einsum("hkv,hlv->kl", p_do, w_uv, preferred_element_type=f32)
    rope_grad = jnp.sum(ds_q[:, :, D_NOPE:], axis=0)
    key_grad = jnp.concatenate([lat_grad, rope_grad], axis=1).astype(bf16)

    with jax.named_scope("sum_heads"):
        parts = lax.all_to_all(key_grad.reshape(heads, CHUNK, lat), "head", 0, 0)
        share = jnp.sum(parts.astype(f32), axis=0)
    token_grad = share[pre : pre + tok].astype(bf16)
    with jax.named_scope("sum_slots"):
        sent = jnp.broadcast_to(share[:pre].astype(bf16)[None], (reqs, pre, lat))
        given = lax.all_to_all(sent, "req", 0, 0)
        owned = (slot_ids == req_place)[:, None, None]
        pool_grad = jnp.sum(jnp.where(owned, given.astype(f32), 0.0), axis=0, keepdims=True)
    return d_queries, token_grad, pool_grad


def solution(mesh):
    return jax.shard_map(
        shards,
        mesh=mesh,
        in_specs=(
            P("req", "head", None),
            P("req", "head", None),
            P("req", None),
            P("head", None, None),
            P("head", None, None),
            P("req", "head", None),
            P(),
            P(),
        ),
        out_specs=(P("req", "head", None), P(("req", "head"), None), P("req", "head", None)),
        check_vma=False,
    )
```

time: 541 us -> 115 us (0.21); the launches traced: 532 us -> 113 us
  waiting for transfers between devices: 342 us -> 40.1 us
  blocking collectives: 136 us -> 0 us
  starting transfers between devices: 0.08 us -> 35.3 us
  between operations: 15.5 us -> 2.78 us
  local copies, waits for them, and re-layouts: 12.1 us -> 6.24 us
    unnamed x3 -> x0, waiting for transfers between devices: 267 us -> none
    unnamed x1 -> x0, blocking collectives: 97.1 us -> none
    all_gather x1 -> x0, waiting for transfers between devices: 75.7 us -> none  [shards(): shard_piece = lax.all_gather(group_rows, 'req', axis=0, tiled=True)]
    all_to_all x0 -> x4, waiting for transfers between devices: none -> 40.1 us  [the longest x1 17.6 us: shards(): parts = lax.all_to_all(key_grad.reshape(heads, CHUNK, lat), 'head', 0, 0)]
    all_gather x1 -> x0, blocking collectives: 39.3 us -> none  [shards(): group_rows = lax.all_gather(pool_half, 'head', axis=1, tiled=True)]
    all_to_all x0 -> x4, starting transfers between devices: none -> 35.3 us  [the longest x1 17.8 us: shards(): all_slots = lax.all_to_all(mine, 'req', 0, 0)]
    dot_general x10 -> x7, matrix products: 11.7 us -> 21.9 us  [the longest x1 6.6 us: shards(): jnp.einsum('hsk,hkn->shn', d_scores, key_full, preferred_element_type=f32)]
    unnamed x25 -> x9, local copies, waits for them, and re-layouts: 8.55 us -> 1.29 us
  transfers between devices with their start and end apart: 2 -> 4, of which waited for: 2 -> 4; matrix products, arithmetic and copies ran while one was open for 3% -> 10% of each run, Pallas kernels for 0% -> 0%
where the time goes in v1:
time: 115 us; the launch traced here: 113 us
  waiting for transfers between devices  40.1 us (35%)
  starting transfers between devices  35.3 us (31%)
  matrix products  21.9 us (19%)
  other arithmetic  7.09 us (6%)
  local copies, waits for them, and re-layouts  6.24 us (5%)
  between operations  2.78 us (2%)
    all_to_all x1, starting transfers between devices, shards(): all_slots = lax.all_to_all(mine, 'req', 0, 0)  17.8 us
    all_to_all x1, waiting for transfers between devices, shards(): parts = lax.all_to_all(key_grad.reshape(heads, CHUNK, lat), 'head', 0, 0)  17.6 us
    all_to_all x1, waiting for transfers between devices, shards(): all_slots = lax.all_to_all(mine, 'req', 0, 0)  8.81 us
    all_to_all x1, waiting for transfers between devices, shards(): given = lax.all_to_all(sent, 'req', 0, 0)  7.62 us
    dot_general x1, matrix products, shards(): jnp.einsum('hsk,hkn->shn', d_scores, key_full, preferred_element_type=f32)  6.6 us
    all_to_all x1, starting transfers between devices, shards(): lax.all_to_all(jnp.broadcast_to(rows, (heads, pre, lat)), 'head', 0, 0)  6.3 us
    all_to_all x1, waiting for transfers between devices, shards(): lax.all_to_all(jnp.broadcast_to(rows, (heads, pre, lat)), 'head', 0, 0)  6.08 us
    dot_general x1, matrix products, shards(): ds_q = jnp.einsum('hsk,hsn->hkn', d_scores, q, preferred_element_type=f32)  5.82 us
  transfers between devices with their start and end apart: 4, of which 4 were waited for; matrix products, arithmetic and copies ran while one was open for 10% of the time, Pallas kernels for 0%

profile of v1, /device:TPU:6, one launch (start us, length us, event | category | flops | bytes accessed | tf_op | source)
XLA Modules:
  0.0 113.4 jit_solution(9190036917629421076)
XLA Ops:
  0.6 0.0 copy-start
  0.6 0.0 copy-start.2
  0.7 0.8 convert_bitcast_fusion
  1.4 0.6 broadcast_in_dim.81
  2.1 17.8 %all-to-all-start = ((bf16[16,2,576]{2,1,0:T(2,128)(2,1)}), bf16[16,2,576]{2,1,0:T(2,128)(2,1)S(1)}, u32[]{:S(2)}, u32[]{:S(2)}) async-start(bf16[16,2,576]{2,1,0:T(2,128)(2,1)} %broadcast_in_dim.81), calls=%async_computation | async-start | bytes 81920 | tf_op jit(solution)/shard_map/fetch_slots/all_to_all | solution.py:28
  19.9 0.7 compare_select_fusion
  20.6 1.3 %gather_fusion = s32[16]{0:T(128)S(1)} fusion(s32[16]{0:T(128)} %param.15, s32[1024]{0:T(1024)S(1)} %pad_clamp_fusion), kind=kCustom, calls=%fused_computation | custom fusion | bytes 192 | tf_op jit(solution)/shard_map/gather | solution.py:19
  21.9 0.6 dynamic_slice.8
  23.8 1.3 %copy.47 = bf16[384,576]{1,0:T(8,128)(2,1)S(1)} copy(bf16[384,576]{0,1:T(8,128)(2,1)} %param.10) | data formatting | bytes 884736 | tf_op args[2]
  25.1 0.1 reshape.72
  25.9 0.1 pad.6.clone
  25.9 8.8 %all-to-all-done = bf16[16,2,576]{2,1,0:T(2,128)(2,1)S(1)} async-done(((bf16[16,2,576]{2,1,0:T(2,128)(2,1)}), bf16[16,2,576]{2,1,0:T(2,128)(2,1)S(1)}, u32[]{:S(2)}, u32[]{:S(2)}) %all-to-all-start) | async-done | bytes 36896 | tf_op jit(solution)/shard_map/fetch_slots/all_to_all | solution.py:28
  34.7 0.7 broadcast_in_dim.84
  35.4 6.3 %all-to-all-start.1 = ((bf16[32,2,576]{2,1,0:T(2,128)(2,1)}), bf16[32,2,576]{2,1,0:T(2,128)(2,1)S(1)}, u32[]{:S(2)}, u32[]{:S(2)}) async-start(bf16[32,2,576]{2,1,0:T(2,128)(2,1)} %broadcast_in_dim.84), calls=%async_computation.1 | async-start | bytes 163840 | tf_op jit(solution)/shard_map/spread_prefix/all_to_all | solution.py:31
  41.8 0.2 iota_compare_fusion
  41.9 6.1 %all-to-all-done.1 = bf16[32,2,576]{2,1,0:T(2,128)(2,1)S(1)} async-done(((bf16[32,2,576]{2,1,0:T(2,128)(2,1)}), bf16[32,2,576]{2,1,0:T(2,128)(2,1)S(1)}, u32[]{:S(2)}, u32[]{:S(2)}) %all-to-all-start.1) | async-done | bytes 73760 | tf_op jit(solution)/shard_map/spread_prefix/all_to_all | solution.py:31
  48.0 0.4 maximum_maximum_fusion
  48.4 0.0 copy-done.2
  48.4 0.5 fusion.21
  48.9 0.1 copy.48
  49.0 0.0 copy-done
  49.0 0.8 fusion.26
  49.8 0.0 copy-start.1
  49.9 0.0 copy-start.3
  49.9 3.3 %fusion.52 = (f32[4,384]{1,0:T(4,128)S(1)}, f32[4,384,512]{1,2,0:T(8,128)}) fusion(f32[4,512,384]{2,1,0:T(8,128)S(1)} %fusion.26, pred[384,512]{0,1:T(8,128)(4,1)S(1)} %iota_compare_fusion), kind=kOutput, calls=%fused_computation.74 | output fusion | flops 5505535 | bytes 6494208 | tf_op jit(solution)/shard_map/sub | solution.py:53
  53.2 0.0 copy-done.1
  53.2 0.0 copy-done.3
  53.2 2.6 %fusion.23 = f32[4,512,384]{2,1,0:T(8,128)} fusion(bf16[4,512,128]{2,1,0:T(8,128)(2,1)S(1)} %copy-done.1, bf16[512,576]{1,0:T(8,128)(2,1)S(1)} %bitcast.81, bf16[4,384,128]{2,0,1:T(4,128)(2,1)S(1)} %bitcast.84), kind=kOutput, calls=%fused_computation.31 | convolution fusion | flops 470024192 | bytes 4587520 | tf_op jit(solution)/shard_map/hsv,hkv->hsk/dot_general | solution.py:56
  55.7 3.7 %convolution_bitcast_fusion = f32[512,512]{1,0:T(8,128)} fusion(bf16[4,512,128]{2,1,0:T(8,128)(2,1)S(1)} %copy-done.1, bf16[4,384,128]{2,0,1:T(4,128)(2,1)S(1)} %bitcast.85, f32[4,384,512]{1,2,0:T(8,128)} %get-tuple-element.4, f32[4,384]{1,0:T(4,128)S(1)} %get-tuple-element.3), kind=kOutput, calls=%fused_computation.20 | convolution fusion | flops 471597056 | bytes 5117952 | tf_op jit(solution)/shard_map/hkv,hlv->kl/dot_general | solution.py:63
  59.5 5.8 %fusion.12 = f32[4,512,192]{1,2,0:T(8,128)S(1)} fusion(f32[4,512,384]{2,1,0:T(8,128)} %fusion.23, bf16[384,4,192]{0,2,1:T(8,128)(2,1)S(1)} %copy-done, f32[4,384,512]{1,2,0:T(8,128)} %get-tuple-element.4, f32[4,384]{1,0:T(4,128)S(1)} %get-tuple-element.3), kind=kOutput, calls=%fused_computation.18 | convolution fusion | flops 307496960 | bytes 8460288 | tf_op jit(solution)/shard_map/hsk,hsn->hkn/dot_general | solution.py:60
  65.4 1.9 %fusion.19 = bf16[512,512]{1,0:T(8,128)(2,1)S(1)} fusion(f32[512,512]{1,0:T(8,128)} %convolution_bitcast_fusion, bf16[4,128,512]{2,1,0:T(8,128)(2,1)} %param.11, f32[4,512,192]{1,2,0:T(8,128)S(1)} %fusion.12), kind=kOutput, calls=%fused_computation.27 | convolution fusion | flops 268959744 | bytes 2621440 | tf_op jit(solution)/shard_map/hkn,hnl->kl/dot_general | solution.py:62
  67.2 0.1 copy.54
  67.4 0.9 pad_maximum_fusion.1
  68.3 5.6 %all-to-all-start.2 = ((bf16[32,16,576]{2,1,0:T(8,128)(2,1)}), bf16[32,16,576]{2,1,0:T(8,128)(2,1)S(1)}, u32[]{:S(2)}, u32[]{:S(2)}) async-start(bf16[32,16,576]{2,1,0:T(8,128)(2,1)} %pad_maximum_fusion.1), calls=%async_computation.2 | async-start | bytes 1310720 | tf_op jit(solution)/shard_map/sum_heads/all_to_all | solution.py:68
  73.9 17.6 %all-to-all-done.2 = bf16[32,16,576]{2,1,0:T(8,128)(2,1)S(1)} async-done(((bf16[32,16,576]{2,1,0:T(8,128)(2,1)}), bf16[32,16,576]{2,1,0:T(8,128)(2,1)S(1)}, u32[]{:S(2)}, u32[]{:S(2)}) %all-to-all-start.2) | async-done | bytes 589856 | tf_op jit(solution)/shard_map/sum_heads/all_to_all | solution.py:68
  91.5 0.1 reduce
  91.6 0.6 broadcast_in_dim.92
  92.3 5.6 %all-to-all-start.3 = ((bf16[16,2,576]{2,1,0:T(2,128)(2,1)}), bf16[16,2,576]{2,1,0:T(2,128)(2,1)S(1)}, u32[]{:S(2)}, u32[]{:S(2)}) async-start(bf16[16,2,576]{2,1,0:T(2,128)(2,1)} %broadcast_in_dim.92), calls=%async_computation.3 | async-start | bytes 81920 | tf_op jit(solution)/shard_map/sum_slots/all_to_all | solution.py:73
  97.9 6.6 %fusion.20 = bf16[384,4,192]{0,2,1:T(8,128)(2,1)} fusion(f32[4,512,384]{2,1,0:T(8,128)} %fusion.23, bf16[4,512,64]{1,2,0:T(8,128)(2,1)S(1)} %broadcast_in_dim.86, bf16[4,512,128]{1,2,0:T(8,128)(2,1)S(1)} %fusion.21, f32[4,384,512]{1,2,0:T(8,128)} %get-tuple-element.4, f32[4,384]{1,0:T(4,128)S(1)} %get-tuple-element.3), kind=kOutput, calls=%fused_computation.28 | convolution fusion | flops 309364736 | bytes 7673856 | tf_op jit(solution)/shard_map/hsk,hkn->shn/dot_general | solution.py:59
  104.5 0.6 slice.33
  105.1 7.6 %all-to-all-done.3 = bf16[16,2,576]{2,1,0:T(2,128)(2,1)S(1)} async-done(((bf16[16,2,576]{2,1,0:T(2,128)(2,1)}), bf16[16,2,576]{2,1,0:T(2,128)(2,1)S(1)}, u32[]{:S(2)}, u32[]{:S(2)}) %all-to-all-start.3) | async-done | bytes 36896 | tf_op jit(solution)/shard_map/sum_slots/all_to_all | solution.py:73
  112.7 0.7 select_reduce_fusion
  (9 shorter events, 0.1 us)
Async XLA Ops:
  0.6 48.4 %copy-start = (bf16[384,4,192]{0,2,1:T(8,128)(2,1)S(1)}, bf16[384,4,192]{0,2,1:T(8,128)(2,1)}, u32[]{:S(2)}) copy-start(bf16[384,4,192]{0,2,1:T(8,128)(2,1)} %param.8) | copy-start | bytes 1769476
  0.6 47.7 %copy-start.2 = (bf16[4,128,512]{2,1,0:T(8,128)(2,1)S(1)}, bf16[4,128,512]{2,1,0:T(8,128)(2,1)}, u32[]{:S(2)}) copy-start(bf16[4,128,512]{2,1,0:T(8,128)(2,1)} %param.11) | copy-start | bytes 1572868
  2.1 32.7 %all-to-all-start = ((bf16[16,2,576]{2,1,0:T(2,128)(2,1)}), bf16[16,2,576]{2,1,0:T(2,128)(2,1)S(1)}, u32[]{:S(2)}, u32[]{:S(2)}) async-start(bf16[16,2,576]{2,1,0:T(2,128)(2,1)} %broadcast_in_dim.81), calls=%async_computation | async-start | bytes 81920 | tf_op jit(solution)/shard_map/fetch_slots/all_to_all | solution.py:28
  35.4 12.6 %all-to-all-start.1 = ((bf16[32,2,576]{2,1,0:T(2,128)(2,1)}), bf16[32,2,576]{2,1,0:T(2,128)(2,1)S(1)}, u32[]{:S(2)}, u32[]{:S(2)}) async-start(bf16[32,2,576]{2,1,0:T(2,128)(2,1)} %broadcast_in_dim.84), calls=%async_computation.1 | async-start | bytes 163840 | tf_op jit(solution)/shard_map/spread_prefix/all_to_all | solution.py:31
  49.8 3.3 %copy-start.1 = (bf16[4,512,128]{2,1,0:T(8,128)(2,1)S(1)}, bf16[4,512,128]{2,1,0:T(8,128)(2,1)}, u32[]{:S(2)}) copy-start(bf16[4,512,128]{2,1,0:T(8,128)(2,1)} %param.12) | copy-start | bytes 1572868
  49.9 3.3 %copy-start.3 = (bf16[384,4,128]{2,1,0:T(4,128)(2,1)S(1)}, bf16[384,4,128]{2,1,0:T(4,128)(2,1)}, u32[]{:S(2)}) copy-start(bf16[384,4,128]{2,1,0:T(4,128)(2,1)} %param.9) | copy-start | bytes 1179652
  68.3 23.2 %all-to-all-start.2 = ((bf16[32,16,576]{2,1,0:T(8,128)(2,1)}), bf16[32,16,576]{2,1,0:T(8,128)(2,1)S(1)}, u32[]{:S(2)}, u32[]{:S(2)}) async-start(bf16[32,16,576]{2,1,0:T(8,128)(2,1)} %pad_maximum_fusion.1), calls=%async_computation.2 | async-start | bytes 1310720 | tf_op jit(solution)/shard_map/sum_heads/all_to_all | solution.py:68
  92.3 20.4 %all-to-all-start.3 = ((bf16[16,2,576]{2,1,0:T(2,128)(2,1)}), bf16[16,2,576]{2,1,0:T(2,128)(2,1)S(1)}, u32[]{:S(2)}, u32[]{:S(2)}) async-start(bf16[16,2,576]{2,1,0:T(2,128)(2,1)} %broadcast_in_dim.92), calls=%async_computation.3 | async-start | bytes 81920 | tf_op jit(solution)/shard_map/sum_slots/all_to_all | solution.py:73

commit v2 on v1

v2 whole, which is shorter than its diff:
```python
import jax
import jax.numpy as jnp
from jax import lax
from jax.experimental import pallas as pl
from jax.experimental.pallas import tpu as pltpu
from jax.sharding import PartitionSpec as P

D_LAT = 512
D_ROPE = 64
D_NOPE = 128
SCALE = float(D_NOPE + D_ROPE) ** (-0.5)
bf16 = jnp.bfloat16
f32 = jnp.float32
CHUNK = 16
IN_VMEM = pl.BlockSpec(memory_space=pltpu.VMEM)
PARAMS = pltpu.CompilerParams(vmem_limit_bytes=24 * 1024 * 1024)


def dot(a, b):
    return jnp.dot(a, b, preferred_element_type=f32)


def dot_nt(a, b):
    return lax.dot_general(a, b, (((1,), (1,)), ((), ())), preferred_element_type=f32)


def dot_tn(a, b):
    return lax.dot_general(a, b, (((0,), (0,)), ((), ())), preferred_element_type=f32)


def token_scores(qt_ref, do_ref, tok_ref, uk_ref, uv_ref, e_ref, dp_ref, key_ref, stat_ref, both_ref):
    both_ref[:D_NOPE] = uk_ref[...]
    both_ref[D_NOPE:] = uv_ref[...].T
    made = dot_nt(tok_ref[:, :D_LAT], both_ref[...]).astype(bf16)
    key = jnp.concatenate([made[:, :D_NOPE], tok_ref[:, D_LAT:]], axis=1)
    key_ref[...] = key
    scores = dot(key, qt_ref[...]) * SCALE
    row = lax.broadcasted_iota(jnp.int32, scores.shape, 0)
    col = lax.broadcasted_iota(jnp.int32, scores.shape, 1)
    scores = jnp.where(row <= col, scores, -1e30)
    top = jnp.max(scores, axis=0, keepdims=True)
    terms = jnp.where(row <= col, jnp.exp(scores - top), 0.0)
    d_probs = dot_nt(made[:, D_NOPE:], do_ref[...])
    e_ref[...] = terms
    dp_ref[...] = d_probs
    stat_ref[0:1] = top
    stat_ref[1:2] = jnp.sum(terms, axis=0, keepdims=True)
    stat_ref[2:3] = jnp.sum(terms * d_probs, axis=0, keepdims=True)


def key_grads(qt_ref, do_ref, pre_ref, both_ref, e_ref, dp_ref, stat_ref, grad_ref, ds_ref, key_ref, tok_acc, pre_acc):
    n_h = qt_ref.shape[0]
    n_pre = pre_ref.shape[0]
    width = both_ref.shape[1]
    both = both_ref[...].reshape(n_h * width, D_LAT)
    made = dot_nt(pre_ref[:, :D_LAT], both).astype(bf16)
    sides = []
    rope = None
    for h in range(n_h):
        key = jnp.concatenate([made[:, h * width : h * width + D_NOPE], pre_ref[:, D_LAT:]], axis=1)
        key_ref[h] = key
        val = made[:, h * width + D_NOPE : (h + 1) * width]
        qt = qt_ref[h]
        do = do_ref[h]
        scores = dot(key, qt) * SCALE
        d_probs = dot_nt(val, do)
        tok_top = stat_ref[h, 0:1]
        top = jnp.maximum(tok_top, jnp.max(scores, axis=0, keepdims=True))
        terms = jnp.exp(scores - top)
        shrink = jnp.exp(tok_top - top)
        inverse = 1.0 / (shrink * stat_ref[h, 1:2] + jnp.sum(terms, axis=0, keepdims=True))
        pre_probs = terms * inverse
        factor = shrink * inverse
        delta = factor * stat_ref[h, 2:3] + jnp.sum(pre_probs * d_probs, axis=0, keepdims=True)
        tok_probs = e_ref[h] * factor
        ds_ref[h, :n_pre] = (pre_probs * (d_probs - delta) * SCALE).astype(bf16)
        ds_ref[h, n_pre:] = (tok_probs * (dp_ref[h] - delta) * SCALE).astype(bf16)
        probs = jnp.concatenate([pre_probs.astype(bf16), tok_probs.astype(bf16)], axis=0)
        ds_q = dot_nt(ds_ref[h], qt)
        sides += [ds_q[:, :D_NOPE].astype(bf16), dot(probs, do).astype(bf16)]
        rope = ds_q[:, D_NOPE:] if rope is None else rope + ds_q[:, D_NOPE:]
    lat = dot(jnp.concatenate(sides, axis=1), both)
    pre_acc[:, :D_LAT] = lat[:n_pre]
    pre_acc[:, D_LAT:] = rope[:n_pre]
    tok_acc[:, :D_LAT] = lat[n_pre:]
    tok_acc[:, D_LAT:] = rope[n_pre:]
    heads, chunk, wide = grad_ref.shape
    pre = n_pre // heads
    tok = tok_acc.shape[0] // heads
    spare = jnp.zeros((chunk - pre - tok, wide), f32)
    for i in range(heads):
        piece = [pre_acc[i * pre : (i + 1) * pre], tok_acc[i * tok : (i + 1) * tok], spare]
        grad_ref[i] = jnp.concatenate(piece, axis=0).astype(bf16)


def query_grads(tok_key_ref, pre_key_ref, ds_ref, out_ref):
    key = jnp.concatenate([pre_key_ref[...], tok_key_ref[...]], axis=0)
    out_ref[...] = dot_tn(key, ds_ref[...]).astype(bf16)


def per_head(*shape):
    return pl.BlockSpec((None, *shape), lambda h: (h, 0, 0))


def shared(*shape):
    return pl.BlockSpec(shape, lambda h: (0, 0))


def struct(shape, dtype):
    return jax.ShapeDtypeStruct(shape, dtype)


def cost(flops, nbytes, exps=0):
    return pl.CostEstimate(flops=int(flops), bytes_accessed=int(nbytes), transcendentals=int(exps))


def shards(queries, d_out, tok_latent, w_uk, w_uv, pool, tenant_of_request, slot_of_tenant):
    heads = lax.axis_size("head")
    reqs = lax.axis_size("req")
    req_place = lax.axis_index("req")
    slot_ids = slot_of_tenant[tenant_of_request]
    my_slot = lax.dynamic_index_in_dim(slot_ids, req_place, 0, keepdims=False)
    lat = pool.shape[2]
    pre = pool.shape[1]
    seq, n_h, d_q = queries.shape
    d_v = d_out.shape[2]
    tok = seq // heads
    n_pre = pre * heads

    with jax.named_scope("fetch_slots"):
        all_slots = lax.all_to_all(jnp.broadcast_to(pool, (reqs, pre, lat)), "req", 0, 0)

    q_t = jnp.transpose(queries, (1, 2, 0))
    do = jnp.transpose(d_out, (1, 0, 2))
    wide = D_NOPE + d_v
    with jax.named_scope("token_scores"):
        terms, d_probs, tok_key, stats, both = pl.pallas_call(
            token_scores,
            grid=(n_h,),
            in_specs=[per_head(d_q, seq), per_head(seq, d_v), shared(seq, lat), per_head(D_NOPE, D_LAT), per_head(D_LAT, d_v)],
            out_specs=[per_head(seq, seq), per_head(seq, seq), per_head(seq, d_q), per_head(8, seq), per_head(wide, D_LAT)],
            out_shape=[
                struct((n_h, seq, seq), f32),
                struct((n_h, seq, seq), f32),
                struct((n_h, seq, d_q), bf16),
                struct((n_h, 8, seq), f32),
                struct((n_h, wide, D_LAT), bf16),
            ],
            compiler_params=PARAMS,
            cost_estimate=cost(n_h * 2.0e8, 8e6, n_h * seq * seq),
        )(q_t, do, tok_latent, w_uk, w_uv)

    with jax.named_scope("spread_prefix"):
        rows = lax.dynamic_index_in_dim(all_slots, my_slot, 0, keepdims=True).astype(bf16)
        prefix = lax.all_to_all(jnp.broadcast_to(rows, (heads, pre, lat)), "head", 0, 0)
        prefix = prefix.reshape(n_pre, lat)

    with jax.named_scope("key_grads"):
        grads, d_scores, pre_key = pl.pallas_call(
            key_grads,
            in_specs=[IN_VMEM] * 7,
            out_specs=[IN_VMEM] * 3,
            out_shape=[
                struct((heads, CHUNK, lat), bf16),
                struct((n_h, n_pre + seq, seq), bf16),
                struct((n_h, n_pre, d_q), bf16),
            ],
            scratch_shapes=[pltpu.VMEM((seq, lat), f32), pltpu.VMEM((n_pre, lat), f32)],
            compiler_params=PARAMS,
            cost_estimate=cost(n_h * 2.5e8, 8e6, n_h * seq * n_pre),
        )(q_t, do, prefix, both, terms, d_probs, stats)

    with jax.named_scope("sum_heads"):
        parts = lax.all_to_all(grads, "head", 0, 0)

    with jax.named_scope("query_grads"):
        d_q_t = pl.pallas_call(
            query_grads,
            grid=(n_h,),
            in_specs=[per_head(seq, d_q), per_head(n_pre, d_q), per_head(n_pre + seq, seq)],
            out_specs=per_head(d_q, seq),
            out_shape=struct((n_h, d_q, seq), bf16),
            compiler_params=PARAMS,
            cost_estimate=cost(n_h * 8e7, 3e6),
        )(tok_key, pre_key, d_scores)
        d_queries = jnp.transpose(d_q_t, (2, 0, 1))

    with jax.named_scope("sum_slots"):
        share = jnp.sum(parts.astype(f32), axis=0)
        token_grad = share[pre : pre + tok].astype(bf16)
        given = lax.all_to_all(jnp.broadcast_to(share[:pre].astype(bf16)[None], (reqs, pre, lat)), "req", 0, 0)
        owned = (slot_ids == req_place)[:, None, None]
        pool_grad = jnp.sum(jnp.where(owned, given.astype(f32), 0.0), axis=0, keepdims=True)
    return d_queries, token_grad, pool_grad


def solution(mesh):
    return jax.shard_map(
        shards,
        mesh=mesh,
        in_specs=(
            P("req", "head", None),
            P("req", "head", None),
            P("req", None),
            P("head", None, None),
            P("head", None, None),
            P("req", "head", None),
            P(),
            P(),
        ),
        out_specs=(P("req", "head", None), P(("req", "head"), None), P("req", "head", None)),
        check_vma=False,
    )
```

time: 115 us -> 114 us (level)
  the two profiles are of different devices: /device:TPU:6 before, /device:TPU:1 now
where the time goes in v2:
time: 114 us; the launch traced here: 113 us
  starting transfers between devices  29.8 us (26%)
  blocking collectives  26.6 us (23%)
  local copies, waits for them, and re-layouts  24.6 us (22%)
  waiting for transfers between devices  20.1 us (18%)
  Pallas kernels  8.12 us (7%)
  between operations  2.69 us (2%)
  other arithmetic  1.5 us (1%)
    all_to_all x1, blocking collectives, shards(): parts = lax.all_to_all(grads, 'head', 0, 0)  26.6 us
    unnamed x36, local copies, waits for them, and re-layouts  18.5 us
    all_to_all x1, starting transfers between devices, shards(): lax.all_to_all(jnp.broadcast_to(pool, (reqs, pre, lat)), 'req', 0, 0)  18.4 us
    all_to_all x1, waiting for transfers between devices, shards(): lax.all_to_all(jnp.broadcast_to(share[:pre].astype(bf16)[None], (reqs, pr...  10.2 us
    all_to_all x1, waiting for transfers between devices, shards(): lax.all_to_all(jnp.broadcast_to(pool, (reqs, pre, lat)), 'req', 0, 0)  9.89 us
    all_to_all x1, starting transfers between devices, shards(): lax.all_to_all(jnp.broadcast_to(rows, (heads, pre, lat)), 'head', 0, 0)  7.89 us
    all_to_all x1, starting transfers between devices, shards(): lax.all_to_all(jnp.broadcast_to(share[:pre].astype(bf16)[None], (reqs, pr...  3.49 us
    pallas_call x1, Pallas kernels, shards(): pl.pallas_call(token_scores, grid=(n_h,), in_specs=[per_head(d_q, seq), p...  3.01 us
  transfers between devices with their start and end apart: 3, of which 2 were waited for; matrix products, arithmetic and copies ran while one was open for 5% of the time, Pallas kernels for 5%

profile of v2, /device:TPU:1, one launch (start us, length us, event | category | flops | bytes accessed | tf_op | source)
XLA Modules:
  0.0 113.5 jit_solution(1313307491891258656)
XLA Ops:
  0.6 0.0 copy-start
  0.6 1.3 %broadcast_in_dim.40 = bf16[16,2,576]{2,1,0:T(2,128)(2,1)} broadcast(f32[2,576]{1,0:T(2,128)} %bitcast.16), dimensions={1,2} | broadcast | bytes 41472 | tf_op jit(solution)/shard_map/fetch_slots/broadcast_in_dim | solution.py:131
  2.0 18.4 %all-to-all-start = ((bf16[16,2,576]{2,1,0:T(2,128)(2,1)}), bf16[16,2,576]{2,1,0:T(2,128)(2,1)S(1)}, u32[]{:S(2)}, u32[]{:S(2)}) async-start(bf16[16,2,576]{2,1,0:T(2,128)(2,1)} %broadcast_in_dim.40), calls=%async_computation | async-start | bytes 81920 | tf_op jit(solution)/shard_map/fetch_slots/all_to_all | solution.py:131
  20.4 0.7 compare_select_fusion
  21.0 0.0 copy-done
  21.0 0.7 gather_fusion
  21.7 0.6 dynamic_slice.8
  24.2 9.9 %all-to-all-done = bf16[16,2,576]{2,1,0:T(2,128)(2,1)S(1)} async-done(((bf16[16,2,576]{2,1,0:T(2,128)(2,1)}), bf16[16,2,576]{2,1,0:T(2,128)(2,1)S(1)}, u32[]{:S(2)}, u32[]{:S(2)}) %all-to-all-start) | async-done | bytes 36896 | tf_op jit(solution)/shard_map/fetch_slots/all_to_all | solution.py:131
  34.1 0.7 broadcast_in_dim.43
  34.8 7.9 %all-to-all-start.1 = ((bf16[32,2,576]{2,1,0:T(2,128)(2,1)}), bf16[32,2,576]{2,1,0:T(2,128)(2,1)}, u32[]{:S(2)}, u32[]{:S(2)}) async-start(bf16[32,2,576]{2,1,0:T(2,128)(2,1)} %broadcast_in_dim.43), calls=%async_computation.1 | async-start | bytes 163840 | tf_op jit(solution)/shard_map/spread_prefix/all_to_all | solution.py:155
  42.7 1.1 copy.22
  43.8 2.0 %copy.18.tok_ref = bf16[384,576]{1,0:T(8,128)(2,1)} copy(bf16[384,576]{0,1:T(8,128)(2,1)} %param.10) | data formatting | bytes 884736 | tf_op args[2]
  45.8 0.0 copy-start.7
  45.8 1.1 copy-done.7
  46.8 0.0 copy-start.9
  46.8 1.0 copy-done.9
  47.9 0.0 copy-start.15
  47.9 1.0 copy-done.15
  48.9 0.0 copy-start.16
  48.9 1.0 copy-done.16
  49.9 3.0 %token_scores.1 = (f32[4,384,384]{2,1,0:T(8,128)S(1)}, f32[4,384,384]{2,1,0:T(8,128)S(1)}, bf16[4,384,192]{2,1,0:T(8,128)(2,1)S(1)}, f32[4,8,384]{2,1,0:T(8,128)S(1)}, bf16[4,256,512]{2,1,0:T(8,128)(2,1)S(1)}) custom-call(bf16[4,192,384]{2,1,0:T(8,128)(2,1)S(1)} %bitcast.12, bf16[4,384,128]{2,1,0:T(8,128)(2,1)S(1)} %bitcast.10, ...), custom_call_target="tpu_custom_call" | custom-call | flops 800000000 | bytes 8000000 | tf_op jit(solution)/shard_map/token_scores/pallas_call | solution.py:137
  53.0 0.0 copy-start.1
  53.0 1.4 %copy-done.1 = f32[4,384,384]{2,1,0:T(8,128)} copy-done((f32[4,384,384]{2,1,0:T(8,128)}, f32[4,384,384]{2,1,0:T(8,128)S(1)}, u32[]{:S(2)}) %copy-start.1) | copy-done | bytes 2359320
  54.4 0.0 copy-start.5
  54.4 1.0 copy-done.5
  55.4 0.6 copy-done.13
  56.0 0.0 all-to-all-done.1
  56.0 1.6 %reshape.13.pre_ref = bf16[64,576]{1,0:T(8,128)(2,1)} reshape(bf16[32,2,576]{2,1,0:T(2,128)(2,1)} %all-to-all-done.1) | data formatting | bytes 147456 | tf_op jit(solution)/shard_map/spread_prefix/reshape | solution.py:156
  57.6 1.7 %copy-done.2 = f32[4,384,384]{2,1,0:T(8,128)S(1)} copy-done((f32[4,384,384]{2,1,0:T(8,128)S(1)}, f32[4,384,384]{2,1,0:T(8,128)}, u32[]{:S(2)}) %copy-start.2) | copy-done | bytes 2359320
  59.2 1.2 %copy-done.6 = bf16[4,256,512]{2,1,0:T(8,128)(2,1)S(1)} copy-done((bf16[4,256,512]{2,1,0:T(8,128)(2,1)S(1)}, bf16[4,256,512]{2,1,0:T(8,128)(2,1)}, u32[]{:S(2)}) %copy-start.6) | copy-done | bytes 1048600
  60.5 1.1 copy-done.8
  61.5 0.9 copy-done.10
  62.4 0.8 copy-done.14
  63.2 2.9 %key_grads.1 = (bf16[32,16,576]{2,1,0:T(8,128)(2,1)S(1)}, bf16[4,448,384]{2,1,0:T(8,128)(2,1)S(1)}, bf16[4,64,192]{2,1,0:T(8,128)(2,1)S(1)}) custom-call(bf16[4,192,384]{2,1,0:T(8,128)(2,1)S(1)} %bitcast.13, bf16[4,384,128]{2,1,0:T(8,128)(2,1)S(1)} %bitcast.11, bf16[64,576]{1,0:T(8,128)(2,1)S(1)} %copy-done.10, bf16[4,256,512]{2,1,0:T(8,128)(2,1)S(1)} %copy-done.6, ...), custom_call_target="tpu_custom_call" | custom-call | flops 1000000000 | bytes 8000000 | tf_op jit(solution)/shard_map/key_grads/pallas_call | solution.py:159
  66.1 0.0 copy-start.3
  66.1 1.1 copy-done.3
  67.2 0.7 copy-done.11
  67.9 26.6 %all_to_all.20 = bf16[32,16,576]{2,1,0:T(8,128)(2,1)S(1)} all-to-all(bf16[32,16,576]{2,1,0:T(8,128)(2,1)S(1)} %get-tuple-element.18), channel_id=1, replica_groups=mesh['req'=16,'head'=32] {'head'}, dimensions={0} | all-to-all | bytes 1179648 | tf_op jit(solution)/shard_map/sum_heads/all_to_all | solution.py:174
  94.5 0.1 reduce
  94.6 0.6 broadcast_in_dim.45
  95.2 3.5 %all-to-all-start.3 = ((bf16[16,2,576]{2,1,0:T(2,128)(2,1)}), bf16[16,2,576]{2,1,0:T(2,128)(2,1)S(1)}, u32[]{:S(2)}, u32[]{:S(2)}) async-start(bf16[16,2,576]{2,1,0:T(2,128)(2,1)} %broadcast_in_dim.45), calls=%async_computation.3 | async-start | bytes 81920 | tf_op jit(solution)/shard_map/sum_slots/all_to_all | solution.py:191
  98.7 0.0 copy-done.4
  98.8 0.0 copy-start.12
  98.8 0.9 copy-done.12
  99.7 2.2 %query_grads.1 = bf16[4,192,384]{2,1,0:T(8,128)(2,1)} custom-call(bf16[4,384,192]{2,1,0:T(8,128)(2,1)S(1)} %get-tuple-element.11.tok_key_ref, bf16[4,64,192]{2,1,0:T(8,128)(2,1)S(1)} %copy-done.12, bf16[4,448,384]{2,1,0:T(8,128)(2,1)S(1)} %copy-done.4), custom_call_target="tpu_custom_call" | custom-call | flops 320000000 | bytes 3000000 | tf_op jit(solution)/shard_map/query_grads/pallas_call | solution.py:177
  101.9 0.6 slice.12
  102.5 10.2 %all-to-all-done.3 = bf16[16,2,576]{2,1,0:T(2,128)(2,1)S(1)} async-done(((bf16[16,2,576]{2,1,0:T(2,128)(2,1)}), bf16[16,2,576]{2,1,0:T(2,128)(2,1)S(1)}, u32[]{:S(2)}, u32[]{:S(2)}) %all-to-all-start.3) | async-done | bytes 36896 | tf_op jit(solution)/shard_map/sum_slots/all_to_all | solution.py:191
  112.7 0.7 select_reduce_fusion
  (12 shorter events, 0.0 us)
Async XLA Ops:
  0.6 20.4 %copy-start = (s32[16]{0:T(128)S(1)}, s32[16]{0:T(128)}, u32[]{:S(2)}) copy-start(s32[16]{0:T(128)} %param.15) | copy-start | bytes 196
  2.0 32.1 %all-to-all-start = ((bf16[16,2,576]{2,1,0:T(2,128)(2,1)}), bf16[16,2,576]{2,1,0:T(2,128)(2,1)S(1)}, u32[]{:S(2)}, u32[]{:S(2)}) async-start(bf16[16,2,576]{2,1,0:T(2,128)(2,1)} %broadcast_in_dim.40), calls=%async_computation | async-start | bytes 81920 | tf_op jit(solution)/shard_map/fetch_slots/all_to_all | solution.py:131
  34.8 21.2 %all-to-all-start.1 = ((bf16[32,2,576]{2,1,0:T(2,128)(2,1)}), bf16[32,2,576]{2,1,0:T(2,128)(2,1)}, u32[]{:S(2)}, u32[]{:S(2)}) async-start(bf16[32,2,576]{2,1,0:T(2,128)(2,1)} %broadcast_in_dim.43), calls=%async_computation.1 | async-start | bytes 163840 | tf_op jit(solution)/shard_map/spread_prefix/all_to_all | solution.py:155
  45.8 1.1 copy-start.7
  46.8 1.0 copy-start.9
  47.9 1.0 copy-start.15
  48.9 1.0 copy-start.16
  53.0 1.4 %copy-start.1 = (f32[4,384,384]{2,1,0:T(8,128)}, f32[4,384,384]{2,1,0:T(8,128)S(1)}, u32[]{:S(2)}) copy-start(f32[4,384,384]{2,1,0:T(8,128)S(1)} %get-tuple-element.14.dp_ref) | copy-start | bytes 7077892
  54.4 1.0 copy-start.5
  55.4 0.6 copy-start.13
  57.6 1.7 %copy-start.2 = (f32[4,384,384]{2,1,0:T(8,128)S(1)}, f32[4,384,384]{2,1,0:T(8,128)}, u32[]{:S(2)}) copy-start(f32[4,384,384]{2,1,0:T(8,128)} %copy-done.1) | copy-start | bytes 7077892
  59.2 1.2 %copy-start.6 = (bf16[4,256,512]{2,1,0:T(8,128)(2,1)S(1)}, bf16[4,256,512]{2,1,0:T(8,128)(2,1)}, u32[]{:S(2)}) copy-start(bf16[4,256,512]{2,1,0:T(8,128)(2,1)} %copy-done.5) | copy-start | bytes 3145732
  60.5 1.1 copy-start.8
  61.5 0.9 copy-start.10
  62.4 0.8 copy-start.14
  66.1 1.1 copy-start.3
  67.2 0.7 copy-start.11
  67.9 30.9 %copy-start.4 = (bf16[4,448,384]{2,1,0:T(8,128)(2,1)S(1)}, bf16[4,448,384]{2,1,0:T(8,128)(2,1)}, u32[]{:S(2)}) copy-start(bf16[4,448,384]{2,1,0:T(8,128)(2,1)} %copy-done.3) | copy-start | bytes 4128772
  95.2 17.5 %all-to-all-start.3 = ((bf16[16,2,576]{2,1,0:T(2,128)(2,1)}), bf16[16,2,576]{2,1,0:T(2,128)(2,1)S(1)}, u32[]{:S(2)}, u32[]{:S(2)}) async-start(bf16[16,2,576]{2,1,0:T(2,128)(2,1)} %broadcast_in_dim.45), calls=%async_computation.3 | async-start | bytes 81920 | tf_op jit(solution)/shard_map/sum_slots/all_to_all | solution.py:191
  98.8 0.9 copy-start.12

commit v3 on v2

--- a/solution.py
+++ b/solution.py
@@ -12,8 +12,9 @@
 bf16 = jnp.bfloat16
 f32 = jnp.float32
 CHUNK = 16
+ANYWHERE = pl.BlockSpec(memory_space=pl.ANY)
 IN_VMEM = pl.BlockSpec(memory_space=pltpu.VMEM)
-PARAMS = pltpu.CompilerParams(vmem_limit_bytes=24 * 1024 * 1024)
+PARAMS = pltpu.CompilerParams(vmem_limit_bytes=56 * 1024 * 1024)
 
 
 def dot(a, b):
@@ -28,7 +29,11 @@
     return lax.dot_general(a, b, (((0,), (0,)), ((), ())), preferred_element_type=f32)
 
 
-def token_scores(qt_ref, do_ref, tok_ref, uk_ref, uv_ref, e_ref, dp_ref, key_ref, stat_ref, both_ref):
+def token_scores(qt_ref, do_ref, tokt_ref, uk_ref, uv_ref, e_ref, dp_ref, key_ref, stat_ref, both_ref, tok_ref):
+    @pl.when(pl.program_id(0) == 0)
+    def _():
+        tok_ref[...] = tokt_ref[...].T
+
     both_ref[:D_NOPE] = uk_ref[...]
     both_ref[D_NOPE:] = uv_ref[...].T
     made = dot_nt(tok_ref[:, :D_LAT], both_ref[...]).astype(bf16)
@@ -48,16 +53,43 @@
     stat_ref[2:3] = jnp.sum(terms * d_probs, axis=0, keepdims=True)
 
 
-def key_grads(qt_ref, do_ref, pre_ref, both_ref, e_ref, dp_ref, stat_ref, grad_ref, ds_ref, key_ref, tok_acc, pre_acc):
+def key_grads(
+    qt_hbm, do_hbm, pre_hbm, both_hbm, e_hbm, dp_hbm, stat_hbm,
+    grad_ref, ds_hbm, key_ref,
+    qt_ref, do_ref, parts_ref, both_ref, e_ref, dp_ref, stat_ref, ds_ref, pre_f32, tok_acc, pre_acc, sems,
+):
     n_h = qt_ref.shape[0]
-    n_pre = pre_ref.shape[0]
+    n_pre = pre_f32.shape[0]
     width = both_ref.shape[1]
+    parts_in = pltpu.make_async_copy(pre_hbm, parts_ref, sems.at[0, 0])
+    both_in = pltpu.make_async_copy(both_hbm, both_ref, sems.at[0, 1])
+    stat_in = pltpu.make_async_copy(stat_hbm, stat_ref, sems.at[0, 2])
+    for copy in (parts_in, both_in, stat_in):
+        copy.start()
+    arrays = ((qt_hbm, qt_ref), (do_hbm, do_ref), (e_hbm, e_ref), (dp_hbm, dp_ref))
+    head_in = [
+        [pltpu.make_async_copy(src.at[h], dst.at[h], sems.at[1 + h, i]) for i, (src, dst) in enumerate(arrays)]
+        for h in range(n_h)
+    ]
+    head_out = [pltpu.make_async_copy(ds_ref.at[h], ds_hbm.at[h], sems.at[1 + h, 4]) for h in range(n_h)]
+    for copies in head_in:
+        for copy in copies:
+            copy.start()
+    heads, pre, wide = parts_ref.shape
+    parts_in.wait()
+    for i in range(heads):
+        pre_f32[i * pre : (i + 1) * pre] = parts_ref[i].astype(f32)
+    prefix = pre_f32[...].astype(bf16)
+    both_in.wait()
     both = both_ref[...].reshape(n_h * width, D_LAT)
-    made = dot_nt(pre_ref[:, :D_LAT], both).astype(bf16)
+    made = dot_nt(prefix[:, :D_LAT], both).astype(bf16)
+    stat_in.wait()
     sides = []
     rope = None
     for h in range(n_h):
-        key = jnp.concatenate([made[:, h * width : h * width + D_NOPE], pre_ref[:, D_LAT:]], axis=1)
+        for copy in head_in[h]:
+            copy.wait()
+        key = jnp.concatenate([made[:, h * width : h * width + D_NOPE], prefix[:, D_LAT:]], axis=1)
         key_ref[h] = key
         val = made[:, h * width + D_NOPE : (h + 1) * width]
         qt = qt_ref[h]
@@ -75,6 +107,7 @@
         tok_probs = e_ref[h] * factor
         ds_ref[h, :n_pre] = (pre_probs * (d_probs - delta) * SCALE).astype(bf16)
         ds_ref[h, n_pre:] = (tok_probs * (dp_ref[h] - delta) * SCALE).astype(bf16)
+        head_out[h].start()
         probs = jnp.concatenate([pre_probs.astype(bf16), tok_probs.astype(bf16)], axis=0)
         ds_q = dot_nt(ds_ref[h], qt)
         sides += [ds_q[:, :D_NOPE].astype(bf16), dot(probs, do).astype(bf16)]
@@ -84,13 +117,14 @@
     pre_acc[:, D_LAT:] = rope[:n_pre]
     tok_acc[:, :D_LAT] = lat[n_pre:]
     tok_acc[:, D_LAT:] = rope[n_pre:]
-    heads, chunk, wide = grad_ref.shape
-    pre = n_pre // heads
+    chunk = grad_ref.shape[1]
     tok = tok_acc.shape[0] // heads
     spare = jnp.zeros((chunk - pre - tok, wide), f32)
     for i in range(heads):
         piece = [pre_acc[i * pre : (i + 1) * pre], tok_acc[i * tok : (i + 1) * tok], spare]
         grad_ref[i] = jnp.concatenate(piece, axis=0).astype(bf16)
+    for copy in head_out:
+        copy.wait()
 
 
 def query_grads(tok_key_ref, pre_key_ref, ds_ref, out_ref):
@@ -137,7 +171,7 @@
         terms, d_probs, tok_key, stats, both = pl.pallas_call(
             token_scores,
             grid=(n_h,),
-            in_specs=[per_head(d_q, seq), per_head(seq, d_v), shared(seq, lat), per_head(D_NOPE, D_LAT), per_head(D_LAT, d_v)],
+            in_specs=[per_head(d_q, seq), per_head(seq, d_v), shared(lat, seq), per_head(D_NOPE, D_LAT), per_head(D_LAT, d_v)],
             out_specs=[per_head(seq, seq), per_head(seq, seq), per_head(seq, d_q), per_head(8, seq), per_head(wide, D_LAT)],
             out_shape=[
                 struct((n_h, seq, seq), f32),
@@ -146,26 +180,40 @@
                 struct((n_h, 8, seq), f32),
                 struct((n_h, wide, D_LAT), bf16),
             ],
+            scratch_shapes=[pltpu.VMEM((seq, lat), bf16)],
             compiler_params=PARAMS,
             cost_estimate=cost(n_h * 2.0e8, 8e6, n_h * seq * seq),
-        )(q_t, do, tok_latent, w_uk, w_uv)
+        )(q_t, do, tok_latent.T, w_uk, w_uv)
 
     with jax.named_scope("spread_prefix"):
         rows = lax.dynamic_index_in_dim(all_slots, my_slot, 0, keepdims=True).astype(bf16)
+        rows, stats = lax.optimization_barrier((rows, stats))
         prefix = lax.all_to_all(jnp.broadcast_to(rows, (heads, pre, lat)), "head", 0, 0)
-        prefix = prefix.reshape(n_pre, lat)
 
     with jax.named_scope("key_grads"):
         grads, d_scores, pre_key = pl.pallas_call(
             key_grads,
-            in_specs=[IN_VMEM] * 7,
-            out_specs=[IN_VMEM] * 3,
+            in_specs=[ANYWHERE] * 7,
+            out_specs=[IN_VMEM, ANYWHERE, IN_VMEM],
             out_shape=[
                 struct((heads, CHUNK, lat), bf16),
                 struct((n_h, n_pre + seq, seq), bf16),
                 struct((n_h, n_pre, d_q), bf16),
             ],
-            scratch_shapes=[pltpu.VMEM((seq, lat), f32), pltpu.VMEM((n_pre, lat), f32)],
+            scratch_shapes=[
+                pltpu.VMEM((n_h, d_q, seq), bf16),
+                pltpu.VMEM((n_h, seq, d_v), bf16),
+                pltpu.VMEM((heads, pre, lat), bf16),
+                pltpu.VMEM((n_h, wide, D_LAT), bf16),
+                pltpu.VMEM((n_h, seq, seq), f32),
+                pltpu.VMEM((n_h, seq, seq), f32),
+                pltpu.VMEM((n_h, 8, seq), f32),
+                pltpu.VMEM((n_h, n_pre + seq, seq), bf16),
+                pltpu.VMEM((n_pre, lat), f32),
+                pltpu.VMEM((seq, lat), f32),
+                pltpu.VMEM((n_pre, lat), f32),
+                pltpu.SemaphoreType.DMA((1 + n_h, 5)),
+            ],
             compiler_params=PARAMS,
             cost_estimate=cost(n_h * 2.5e8, 8e6, n_h * seq * n_pre),
         )(q_t, do, prefix, both, terms, d_probs, stats)

time: 114 us -> 107 us (0.939)
  the two profiles are of different devices: /device:TPU:1 before, /device:TPU:6 now
where the time goes in v3:
time: 107 us; the launch traced here: 105 us
  blocking collectives  35.7 us (33%)
  starting transfers between devices  29.8 us (28%)
  Pallas kernels  16.9 us (16%)
  waiting for transfers between devices  12.6 us (12%)
  local copies, waits for them, and re-layouts  5.7 us (5%)
  between operations  2.64 us (2%)
  other arithmetic  1.5 us (1%)
    all_to_all x1, blocking collectives, shards(): parts = lax.all_to_all(grads, 'head', 0, 0)  23.2 us
    all_to_all x1, starting transfers between devices, shards(): lax.all_to_all(jnp.broadcast_to(pool, (reqs, pre, lat)), 'req', 0, 0)  17.8 us
    all_to_all x1, blocking collectives, shards(): lax.all_to_all(jnp.broadcast_to(rows, (heads, pre, lat)), 'head', 0, 0)  12.5 us
    all_to_all x1, starting transfers between devices, shards(): lax.all_to_all(jnp.broadcast_to(share[:pre].astype(bf16)[None], (reqs, pr...  12 us
    all_to_all x1, waiting for transfers between devices, shards(): lax.all_to_all(jnp.broadcast_to(share[:pre].astype(bf16)[None], (reqs, pr...  10.1 us
    pallas_call x1, Pallas kernels, shards(): pl.pallas_call(token_scores, grid=(n_h,), in_specs=[per_head(d_q, seq), p...  6.67 us
    pallas_call x1, Pallas kernels, shards(): pl.pallas_call(key_grads, in_specs=[ANYWHERE] * 7, out_specs=[IN_VMEM, AN...  6.12 us
    pallas_call x1, Pallas kernels, shards(): pl.pallas_call(query_grads, grid=(n_h,), in_specs=[per_head(seq, d_q), pe...  4.12 us
  transfers between devices with their start and end apart: 2, of which 2 were waited for; matrix products, arithmetic and copies ran while one was open for 4% of the time, Pallas kernels for 10%

profile of v3, /device:TPU:6, one launch (start us, length us, event | category | flops | bytes accessed | tf_op | source)
XLA Modules:
  0.0 104.8 jit_solution(3166100038084083305)
XLA Ops:
  0.6 0.0 copy-start
  0.6 1.3 %broadcast_in_dim.40 = bf16[16,2,576]{2,1,0:T(2,128)(2,1)} broadcast(f32[2,576]{1,0:T(2,128)} %bitcast.17), dimensions={1,2} | broadcast | bytes 41472 | tf_op jit(solution)/shard_map/fetch_slots/broadcast_in_dim | solution.py:165
  2.0 17.8 %all-to-all-start = ((bf16[16,2,576]{2,1,0:T(2,128)(2,1)}), bf16[16,2,576]{2,1,0:T(2,128)(2,1)S(1)}, u32[]{:S(2)}, u32[]{:S(2)}) async-start(bf16[16,2,576]{2,1,0:T(2,128)(2,1)} %broadcast_in_dim.40), calls=%async_computation | async-start | bytes 81920 | tf_op jit(solution)/shard_map/fetch_slots/all_to_all | solution.py:165
  19.8 0.7 compare_select_fusion
  20.5 0.0 copy-done
  20.5 0.7 gather_fusion
  21.1 0.6 dynamic_slice.8
  23.0 1.8 %copy.18 = bf16[384,4,128]{2,0,1:T(8,128)(2,1)} copy(bf16[384,4,128]{2,1,0:T(4,128)(2,1)} %param.9) | data formatting | bytes 786432 | tf_op args[1]
  25.5 6.7 %token_scores.1 = (f32[4,384,384]{2,1,0:T(8,128)}, f32[4,384,384]{2,1,0:T(8,128)}, bf16[4,384,192]{2,1,0:T(8,128)(2,1)}, f32[4,8,384]{2,1,0:T(8,128)}, bf16[4,256,512]{2,1,0:T(8,128)(2,1)}) custom-call(bf16[4,192,384]{2,1,0:T(8,128)(2,1)} %bitcast.12, bf16[4,384,128]{2,1,0:T(8,128)(2,1)} %bitcast.10, bf16[576,384]{1,0:T(8,128)(2,1)} %bitcast.18, ...), custom_call_target="tpu_custom_call" | custom-call | flops 800000000 | bytes 8000000 | tf_op jit(solution)/shard_map/token_scores/pallas_call | solution.py:171
  32.2 2.5 %all-to-all-done = bf16[16,2,576]{2,1,0:T(2,128)(2,1)S(1)} async-done(((bf16[16,2,576]{2,1,0:T(2,128)(2,1)}), bf16[16,2,576]{2,1,0:T(2,128)(2,1)S(1)}, u32[]{:S(2)}, u32[]{:S(2)}) %all-to-all-start) | async-done | bytes 36896 | tf_op jit(solution)/shard_map/fetch_slots/all_to_all | solution.py:165
  34.7 12.5 %all_to_all.20.pre_hbm = bf16[32,2,576]{2,1,0:T(2,128)(2,1)} all-to-all(bf16[32,2,576]{2,1,0:T(2,128)(2,1)S(1)} %broadcast_in_dim.43), channel_id=1, replica_groups=mesh['req'=16,'head'=32] {'head'}, dimensions={0} | all-to-all | bytes 147456 | tf_op jit(solution)/shard_map/spread_prefix/all_to_all | solution.py:191
  47.2 6.1 %key_grads.1 = (bf16[32,16,576]{2,1,0:T(8,128)(2,1)}, bf16[4,448,384]{2,1,0:T(8,128)(2,1)}, bf16[4,64,192]{2,1,0:T(8,128)(2,1)}) custom-call(bf16[4,192,384]{2,1,0:T(8,128)(2,1)} %bitcast.13, bf16[4,384,128]{2,1,0:T(8,128)(2,1)} %bitcast.11, bf16[32,2,576]{2,1,0:T(2,128)(2,1)} %all_to_all.20.pre_hbm, bf16[4,256,512]{2,1,0:T(8,128)(2,1)} %get-tuple-element.16.both_hbm, ...), custom_call_target="tpu_custom_call" | custom-call | flops 1000000000 | bytes 8000000 | tf_op jit(solution)/shard_map/key_grads/pallas_call | solution.py:194
  53.3 23.2 %all_to_all.21 = bf16[32,16,576]{2,1,0:T(8,128)(2,1)S(1)} all-to-all(bf16[32,16,576]{2,1,0:T(8,128)(2,1)} %get-tuple-element.22), channel_id=1, replica_groups=mesh['req'=16,'head'=32] {'head'}, dimensions={0} | all-to-all | bytes 1179648 | tf_op jit(solution)/shard_map/sum_heads/all_to_all | solution.py:222
  76.5 0.1 reduce
  76.6 0.6 broadcast_in_dim.45
  77.3 12.0 %all-to-all-start.3 = ((bf16[16,2,576]{2,1,0:T(2,128)(2,1)}), bf16[16,2,576]{2,1,0:T(2,128)(2,1)S(1)}, u32[]{:S(2)}, u32[]{:S(2)}) async-start(bf16[16,2,576]{2,1,0:T(2,128)(2,1)} %broadcast_in_dim.45), calls=%async_computation.3 | async-start | bytes 81920 | tf_op jit(solution)/shard_map/sum_slots/all_to_all | solution.py:239
  89.3 4.1 %query_grads.1 = bf16[4,192,384]{2,1,0:T(8,128)(2,1)} custom-call(bf16[4,384,192]{2,1,0:T(8,128)(2,1)} %get-tuple-element.13.tok_key_ref, bf16[4,64,192]{2,1,0:T(8,128)(2,1)} %get-tuple-element.20.pre_key_ref, bf16[4,448,384]{2,1,0:T(8,128)(2,1)} %get-tuple-element.21.ds_ref), custom_call_target="tpu_custom_call" | custom-call | flops 320000000 | bytes 3000000 | tf_op jit(solution)/shard_map/query_grads/pallas_call | solution.py:225
  93.4 0.6 slice.12
  94.0 10.1 %all-to-all-done.3 = bf16[16,2,576]{2,1,0:T(2,128)(2,1)S(1)} async-done(((bf16[16,2,576]{2,1,0:T(2,128)(2,1)}), bf16[16,2,576]{2,1,0:T(2,128)(2,1)S(1)}, u32[]{:S(2)}, u32[]{:S(2)}) %all-to-all-start.3) | async-done | bytes 36896 | tf_op jit(solution)/shard_map/sum_slots/all_to_all | solution.py:239
  104.1 0.7 select_reduce_fusion
  (5 shorter events, 0.1 us)
Async XLA Ops:
  0.6 19.9 %copy-start = (s32[16]{0:T(128)S(1)}, s32[16]{0:T(128)}, u32[]{:S(2)}) copy-start(s32[16]{0:T(128)} %param.15) | copy-start | bytes 196
  2.0 32.7 %all-to-all-start = ((bf16[16,2,576]{2,1,0:T(2,128)(2,1)}), bf16[16,2,576]{2,1,0:T(2,128)(2,1)S(1)}, u32[]{:S(2)}, u32[]{:S(2)}) async-start(bf16[16,2,576]{2,1,0:T(2,128)(2,1)} %broadcast_in_dim.40), calls=%async_computation | async-start | bytes 81920 | tf_op jit(solution)/shard_map/fetch_slots/all_to_all | solution.py:165
  77.3 26.8 %all-to-all-start.3 = ((bf16[16,2,576]{2,1,0:T(2,128)(2,1)}), bf16[16,2,576]{2,1,0:T(2,128)(2,1)S(1)}, u32[]{:S(2)}, u32[]{:S(2)}) async-start(bf16[16,2,576]{2,1,0:T(2,128)(2,1)} %broadcast_in_dim.45), calls=%async_computation.3 | async-start | bytes 81920 | tf_op jit(solution)/shard_map/sum_slots/all_to_all | solution.py:239

commit v4 on v1

v4 whole, which is shorter than its diff:
```python
import jax
import jax.numpy as jnp
from jax import lax
from jax.experimental import pallas as pl
from jax.experimental.pallas import tpu as pltpu
from jax.sharding import PartitionSpec as P

D_LAT = 512
D_ROPE = 64
D_NOPE = 128
SCALE = float(D_NOPE + D_ROPE) ** (-0.5)
bf16 = jnp.bfloat16
f32 = jnp.float32
CHUNK = 16
BLOCK = 128
REQ_FIRST = 10
HEAD_FIRST = 20
ANYWHERE = pl.BlockSpec(memory_space=pl.ANY)
IN_VMEM = pl.BlockSpec(memory_space=pltpu.VMEM)
PARAMS = pltpu.CompilerParams(vmem_limit_bytes=24 * 1024 * 1024)


def dot(a, b):
    return jnp.dot(a, b, preferred_element_type=f32)


def dot_nt(a, b):
    return lax.dot_general(a, b, (((1,), (1,)), ((), ())), preferred_element_type=f32)


def dot_tn(a, b):
    return lax.dot_general(a, b, (((0,), (0,)), ((), ())), preferred_element_type=f32)


def project_tokens(qt_hbm, do_hbm, tokt_hbm, uk_hbm, uv_hbm, held_ref, tokt_ref, uv_ref, sems):
    n_h, _, d_v = uv_ref.shape
    seq = tokt_ref.shape[1]
    rows = rows_held(n_h, seq)
    copies = [
        pltpu.make_async_copy(tokt_hbm, tokt_ref, sems.at[0]),
        pltpu.make_async_copy(uk_hbm, held_ref.at[rows["uk"]], sems.at[1]),
        pltpu.make_async_copy(uv_hbm, uv_ref, sems.at[2]),
        pltpu.make_async_copy(do_hbm, held_ref.at[rows["do"]], sems.at[3]),
        pltpu.make_async_copy(qt_hbm, held_ref.at[rows["q"], :seq], sems.at[4]),
    ]
    for copy in copies:
        copy.start()
    copies[0].wait()
    tok = tokt_ref[...].T
    copies[1].wait()
    held_ref[rows["key"]] = dot_nt(tok[:, :D_LAT], held_ref[rows["uk"]]).astype(bf16)
    copies[2].wait()
    at = rows["uv"].start
    for h in range(n_h):
        mine = slice(h * d_v, (h + 1) * d_v)
        held_ref[at + h * d_v : at + (h + 1) * d_v] = uv_ref[h].T
        held_ref[rows["val"], mine] = dot(tok[:, :D_LAT], uv_ref[h]).astype(bf16)
    for copy in copies[3:]:
        copy.wait()
    at = rows["q"].start
    held_ref[at : at + seq, seq : seq + D_ROPE] = tok[:, D_LAT:]


def rows_held(n_h, seq):
    sizes = dict(uk=n_h * D_NOPE, uv=n_h * D_NOPE, do=seq, key=seq, val=seq, q=n_h * (D_NOPE + D_ROPE))
    places, at = {}, 0
    for name, size in sizes.items():
        places[name] = slice(at, at + size)
        at += size
    return places


def key_grads(
    parts_ref, held_ref,
    own_ref, other_ref, ds_hbm, key_hbm,
    ds_ref, key_ref, probs_ref, pre_f32, tok_acc, pre_acc, sems,
):
    n_h, n_keys, seq = ds_ref.shape
    heads, pre, wide = parts_ref.shape
    n_pre = n_keys - seq
    d_q = D_NOPE + D_ROPE
    rows = rows_held(n_h, seq)
    at_q = rows["q"].start
    row = lax.broadcasted_iota(jnp.int32, (BLOCK, BLOCK), 0)
    col = lax.broadcasted_iota(jnp.int32, (BLOCK, BLOCK), 1)
    for i in range(heads):
        pre_f32[i * pre : (i + 1) * pre] = parts_ref[i].astype(f32)
    prefix = pre_f32[...].astype(bf16)
    uk = held_ref[rows["uk"]]
    uv = held_ref[rows["uv"]]
    pre_keys = dot_nt(prefix[:, :D_LAT], uk).astype(bf16)
    pre_vals = dot_nt(prefix[:, :D_LAT], uv).astype(bf16)
    key_rope = jnp.concatenate([prefix[:, D_LAT:], held_ref[at_q : at_q + seq, seq : seq + D_ROPE]], axis=0)
    key_sides = []
    val_sides = []
    rope = None
    out = []
    for h in range(n_h):
        mine = slice(h * D_NOPE, (h + 1) * D_NOPE)
        q_rows = slice(at_q + h * d_q, at_q + (h + 1) * d_q)
        key_ref[h, :, :D_NOPE] = jnp.concatenate([pre_keys[:, mine], held_ref[rows["key"], mine]], axis=0)
        key_ref[h, :, D_NOPE:] = key_rope
        val = jnp.concatenate([pre_vals[:, mine], held_ref[rows["val"], mine]], axis=0)
        for at in range(0, seq, BLOCK):
            here = slice(at, at + BLOCK)
            seen = n_pre + at + BLOCK
            scores = dot(key_ref[h, :seen], held_ref[q_rows, here]) * SCALE
            edge = jnp.where(row <= col, scores[seen - BLOCK :], -1e30)
            scores = jnp.concatenate([scores[: seen - BLOCK], edge], axis=0)
            d_probs = dot_nt(val[:seen], held_ref[rows["do"], mine][here])
            terms = jnp.exp(scores - jnp.max(scores, axis=0, keepdims=True))
            probs = terms * (1.0 / jnp.sum(terms, axis=0, keepdims=True))
            delta = jnp.sum(probs * d_probs, axis=0, keepdims=True)
            probs_ref[h, :seen, here] = probs.astype(bf16)
            ds_ref[h, :seen, here] = (probs * (d_probs - delta) * SCALE).astype(bf16)
            if seen < n_keys:
                probs_ref[h, seen:, here] = jnp.zeros((n_keys - seen, BLOCK), bf16)
                ds_ref[h, seen:, here] = jnp.zeros((n_keys - seen, BLOCK), bf16)
        for i, (kept, target) in enumerate(((key_ref, key_hbm), (ds_ref, ds_hbm))):
            out.append(pltpu.make_async_copy(kept.at[h], target.at[h], sems.at[h, i]))
            out[-1].start()
        ds_q = dot_nt(ds_ref[h], held_ref[q_rows, :seq])
        key_sides.append(ds_q[:, :D_NOPE].astype(bf16))
        val_sides.append(dot(probs_ref[h], held_ref[rows["do"], mine]).astype(bf16))
        rope = ds_q[:, D_NOPE:] if rope is None else rope + ds_q[:, D_NOPE:]
    lat = dot(jnp.concatenate(key_sides, axis=1), uk) + dot(jnp.concatenate(val_sides, axis=1), uv)
    pre_acc[:, :D_LAT] = lat[:n_pre]
    pre_acc[:, D_LAT:] = rope[:n_pre]
    tok_acc[:, :D_LAT] = lat[n_pre:]
    tok_acc[:, D_LAT:] = rope[n_pre:]
    shares, chunk, _ = own_ref.shape
    tok = seq // heads
    spare = jnp.zeros((chunk - pre - tok, wide), f32)
    first_core = lax.rem(lax.axis_index("head"), 2) == 0
    for i in range(shares):
        pair = []
        for core in range(2):
            j = (HEAD_FIRST + 2 * i + core) % heads
            k = (2 * i + core) * pre
            piece = [pre_acc[k : k + pre], tok_acc[j * tok : (j + 1) * tok], spare]
            pair.append(jnp.concatenate(piece, axis=0))
        own_ref[i] = jnp.where(first_core, pair[0], pair[1]).astype(bf16)
        other_ref[i] = jnp.where(first_core, pair[1], pair[0]).astype(bf16)
    for copy in out:
        copy.wait()


def query_grads(key_ref, ds_ref, out_ref):
    out_ref[...] = dot_tn(key_ref[...], ds_ref[...]).astype(bf16)


def per_head(*shape):
    return pl.BlockSpec((None, *shape), lambda h: (h, 0, 0))


def keep(space, *arrays):
    return [pltpu.with_memory_space_constraint(x, space) for x in arrays]


def struct(shape, dtype):
    return jax.ShapeDtypeStruct(shape, dtype)


def cost(flops, nbytes, exps=0):
    return pl.CostEstimate(flops=int(flops), bytes_accessed=int(nbytes), transcendentals=int(exps))


def from_first(first, size):
    return [[(first + i) % size for i in range(size)]]


def shards(queries, d_out, tok_latent, w_uk, w_uv, pool, tenant_of_request, slot_of_tenant):
    heads = lax.axis_size("head")
    reqs = lax.axis_size("req")
    req_first = REQ_FIRST % reqs
    req_group = from_first(req_first, reqs)
    head_group = from_first(HEAD_FIRST % heads, heads)
    req_place = lax.axis_index("req")
    slot_ids = slot_of_tenant.at[tenant_of_request].get(mode="promise_in_bounds")
    my_slot = lax.dynamic_slice(slot_ids, (req_place,), (1,), allow_negative_indices=False)[0]
    lat = pool.shape[2]
    pre = pool.shape[1]
    seq, n_h, d_q = queries.shape
    d_v = d_out.shape[2]
    tok = seq // heads
    n_pre = pre * heads

    with jax.named_scope("fetch_slots"):
        mine = jnp.broadcast_to(pool, (reqs, pre, lat))
        all_slots = lax.all_to_all(mine, "req", 0, 0, axis_index_groups=req_group)

    q_t = jnp.transpose(queries, (1, 2, 0))
    with jax.named_scope("spread_prefix"):
        place = lax.rem(my_slot + (reqs - req_first), reqs)
        rows = lax.dynamic_slice(all_slots, (place, 0, 0), (1, pre, lat), allow_negative_indices=False).astype(bf16)
        rows, d_out = lax.optimization_barrier((rows, d_out))
        prefix = lax.all_to_all(jnp.broadcast_to(rows, (heads, pre, lat)), "head", 0, 0, axis_index_groups=head_group)

    with jax.named_scope("project_tokens"):
        n_rows = max(x.stop for x in rows_held(n_h, seq).values())
        inputs = q_t.reshape(n_h * d_q, seq), d_out.reshape(seq, n_h * d_v), tok_latent.T, w_uk.reshape(n_h * D_NOPE, D_LAT), w_uv
        held = pl.pallas_call(
            project_tokens,
            in_specs=[ANYWHERE] * 5,
            out_specs=IN_VMEM,
            out_shape=pltpu.VMEM((n_rows, D_LAT), bf16),
            scratch_shapes=[
                pltpu.VMEM((lat, seq), bf16),
                pltpu.VMEM((n_h, D_LAT, d_v), bf16),
                pltpu.SemaphoreType.DMA((5,)),
            ],
            compiler_params=PARAMS,
            cost_estimate=cost(n_h * 1.0e8, 5e6),
        )(*keep(pltpu.HBM, *inputs))

    with jax.named_scope("key_grads"):
        own, other, d_scores, keys = pl.pallas_call(
            key_grads,
            in_specs=[IN_VMEM] * 2,
            out_specs=[IN_VMEM, IN_VMEM, ANYWHERE, ANYWHERE],
            out_shape=[
                pltpu.HBM((heads // 2, CHUNK, lat), bf16),
                pltpu.HBM((heads // 2, CHUNK, lat), bf16),
                pltpu.HBM((n_h, n_pre + seq, seq), bf16),
                pltpu.HBM((n_h, n_pre + seq, d_q), bf16),
            ],
            scratch_shapes=[
                pltpu.VMEM((n_h, n_pre + seq, seq), bf16),
                pltpu.VMEM((n_h, n_pre + seq, d_q), bf16),
                pltpu.VMEM((n_h, n_pre + seq, seq), bf16),
                pltpu.VMEM((n_pre, lat), f32),
                pltpu.VMEM((seq, lat), f32),
                pltpu.VMEM((n_pre, lat), f32),
                pltpu.SemaphoreType.DMA((n_h, 2)),
            ],
            compiler_params=PARAMS,
            cost_estimate=cost(n_h * 2.5e8, 5e6, n_h * seq * seq),
        )(prefix, *keep(pltpu.VMEM, held))

    with jax.named_scope("sum_heads"):
        given = lax.ppermute(other, "head", [(i, i ^ 1) for i in range(heads)])
        summed = (own.astype(f32) + given.astype(f32)).astype(bf16)
        core_groups = [[i + core for i in head_group[0][::2]] for core in range(2)]
        parts = lax.all_to_all(summed, "head", 0, 0, axis_index_groups=core_groups)

    with jax.named_scope("query_grads"):
        d_q_t = pl.pallas_call(
            query_grads,
            grid=(n_h,),
            in_specs=[per_head(n_pre + seq, d_q), per_head(n_pre + seq, seq)],
            out_specs=per_head(d_q, seq),
            out_shape=struct((n_h, d_q, seq), bf16),
            compiler_params=PARAMS,
            cost_estimate=cost(n_h * 8e7, 3e6),
        )(*keep(pltpu.HBM, keys, d_scores))

    with jax.named_scope("sum_slots"):
        share = jnp.sum(parts.astype(f32), axis=0)
        token_grad = share[pre : pre + tok].astype(bf16)
        owned = jnp.roll(slot_ids, -req_first) == req_place
        sent, d_q_t, owned = lax.optimization_barrier((share[:pre].astype(bf16), d_q_t, owned))
        sent = jnp.broadcast_to(sent[None], (reqs, pre, lat))
        given = lax.all_to_all(sent, "req", 0, 0, axis_index_groups=req_group)
        pool_grad = jnp.sum(jnp.where(owned[:, None, None], given.astype(f32), 0.0), axis=0, keepdims=True)
    d_queries = jnp.transpose(d_q_t, (2, 0, 1))
    return d_queries, token_grad, pool_grad


def solution(mesh):
    return jax.shard_map(
        shards,
        mesh=mesh,
        in_specs=(
            P("req", "head", None),
            P("req", "head", None),
            P("req", None),
            P("head", None, None),
            P("head", None, None),
            P("req", "head", None),
            P(),
            P(),
        ),
        out_specs=(P("req", "head", None), P(("req", "head"), None), P("req", "head", None)),
        check_vma=False,
    )
```

time: 115 us -> 83.7 us (0.73)
  waiting for transfers between devices: 40.1 us -> 10.9 us
  matrix products: 21.9 us -> 0 us
  starting transfers between devices: 35.3 us -> 49.3 us
  Pallas kernels: 0 us -> 11.7 us
  other arithmetic: 7.09 us -> 3.3 us
  between operations: 2.78 us -> 1.35 us
    all_to_all x4, waiting for transfers between devices: 40.1 us -> 9.24 us  [the longest x1 5.94 us: shards(): parts = lax.all_to_all(summed, 'head', 0, 0, axis_index_groups=core_groups)]
    dot_general x7 -> x0, matrix products: 21.9 us -> none  [the longest x1 6.6 us: shards(): jnp.einsum('hsk,hkn->shn', d_scores, key_full, preferred_element_type=f32)]
    all_to_all x4, starting transfers between devices: 35.3 us -> 47.3 us  [the longest x1 20.8 us: shards(): all_slots = lax.all_to_all(mine, 'req', 0, 0, axis_index_groups=req_group)]
    pallas_call x0 -> x3, Pallas kernels: none -> 11.7 us  [the longest x1 5.39 us: shards(): pl.pallas_call(key_grads, in_specs=[IN_VMEM] * 2, out_specs=[IN_VMEM, IN_...]
    sub x1 -> x0, other arithmetic: 3.31 us -> none  [shards(): terms = jnp.where(visible, jnp.exp(scores - top), 0.0)]
    ppermute x0 -> x1, starting transfers between devices: none -> 2.03 us  [shards(): given = lax.ppermute(other, 'head', [(i, i ^ 1) for i in range(heads)])]
    convert_element_type x0 -> x1, other arithmetic: none -> 1.79 us  [shards(): summed = (own.astype(f32) + given.astype(f32)).astype(bf16)]
    ppermute x0 -> x1, waiting for transfers between devices: none -> 1.7 us  [shards(): given = lax.ppermute(other, 'head', [(i, i ^ 1) for i in range(heads)])]
  transfers between devices with their start and end apart: 4 -> 5, of which waited for: 4 -> 4; matrix products, arithmetic and copies ran while one was open for 10% -> 5% of each run, Pallas kernels for 0% -> 8%
where the time goes in v4:
time: 83.7 us; the launch traced here: 83.1 us
  starting transfers between devices  49.3 us (59%)
  Pallas kernels  11.7 us (14%)
  waiting for transfers between devices  10.9 us (13%)
  local copies, waits for them, and re-layouts  6.41 us (8%)
  other arithmetic  3.3 us (4%)
  between operations  1.35 us (2%)
    all_to_all x1, starting transfers between devices, shards(): all_slots = lax.all_to_all(mine, 'req', 0, 0, axis_index_groups=req_group)  20.8 us
    all_to_all x1, starting transfers between devices, shards(): given = lax.all_to_all(sent, 'req', 0, 0, axis_index_groups=req_group)  15.7 us
    all_to_all x1, waiting for transfers between devices, shards(): parts = lax.all_to_all(summed, 'head', 0, 0, axis_index_groups=core_groups)  5.94 us
    all_to_all x1, starting transfers between devices, shards(): parts = lax.all_to_all(summed, 'head', 0, 0, axis_index_groups=core_groups)  5.47 us
    pallas_call x1, Pallas kernels, shards(): pl.pallas_call(key_grads, in_specs=[IN_VMEM] * 2, out_specs=[IN_VMEM, IN_...  5.39 us
    all_to_all x1, starting transfers between devices, shards(): lax.all_to_all(jnp.broadcast_to(rows, (heads, pre, lat)), 'head', 0, 0, a...  5.36 us
    pallas_call x1, Pallas kernels, shards(): pl.pallas_call(query_grads, grid=(n_h,), in_specs=[per_head(n_pre + seq,...  4.1 us
    pallas_call x1, Pallas kernels, shards(): pl.pallas_call(project_tokens, in_specs=[ANYWHERE] * 5, out_specs=IN_VMEM...  2.24 us
  transfers between devices with their start and end apart: 5, of which 4 were waited for; matrix products, arithmetic and copies ran while one was open for 5% of the time, Pallas kernels for 8%

profile of v4, /device:TPU:6, one launch (start us, length us, event | category | flops | bytes accessed | tf_op | source)
XLA Modules:
  0.0 83.1 jit_solution(9421230649066055832)
XLA Ops:
  0.6 0.0 copy-start
  0.6 1.3 %broadcast_in_dim.40 = bf16[16,2,576]{2,1,0:T(2,128)(2,1)} broadcast(f32[2,576]{1,0:T(2,128)} %bitcast.23), dimensions={1,2} | broadcast | bytes 41472 | tf_op jit(solution)/shard_map/fetch_slots/broadcast_in_dim | solution.py:189
  2.0 20.8 %all-to-all-start = ((bf16[16,2,576]{2,1,0:T(2,128)(2,1)}), bf16[16,2,576]{2,1,0:T(2,128)(2,1)S(1)}, u32[]{:S(2)}, u32[]{:S(2)}) async-start(bf16[16,2,576]{2,1,0:T(2,128)(2,1)} %broadcast_in_dim.40), calls=%async_computation | async-start | bytes 81920 | tf_op jit(solution)/shard_map/fetch_slots/all_to_all | solution.py:190
  22.8 0.7 compare_select_fusion
  23.5 0.0 copy-done
  23.5 0.7 gather_fusion
  24.1 0.6 dynamic_slice.6
  25.4 0.0 all-to-all-done
  25.4 0.7 broadcast_in_dim.43
  26.1 5.4 %all-to-all-start.1 = ((bf16[32,2,576]{2,1,0:T(2,128)(2,1)}), bf16[32,2,576]{2,1,0:T(2,128)(2,1)S(1)}, u32[]{:S(2)}, u32[]{:S(2)}) async-start(bf16[32,2,576]{2,1,0:T(2,128)(2,1)} %broadcast_in_dim.43), calls=%async_computation.1 | async-start | bytes 163840 | tf_op jit(solution)/shard_map/spread_prefix/all_to_all | solution.py:197
  31.5 1.8 %copy.15 = bf16[48,8,4,128]{3,1,2,0:T(8,128)(2,1)} copy(bf16[48,8,4,128]{3,2,1,0:T(4,128)(2,1)} %bitcast.20) | data formatting | bytes 786432
  33.3 2.2 %project_tokens.1.held_ref = bf16[2944,512]{1,0:T(8,128)(2,1)S(1)} custom-call(bf16[768,384]{1,0:T(8,128)(2,1)} %bitcast.16, bf16[384,512]{1,0:T(8,128)(2,1)} %bitcast.15, bf16[576,384]{1,0:T(8,128)(2,1)} %bitcast.19, bf16[512,512]{1,0:T(8,128)(2,1)} %bitcast.18, bf16[4,512,128]{2,1,0:T(8,128)(2,1)} %uv_hbm.1), custom_call_target="tpu_custom_call" | custom-call | flops 400000000 | bytes 5000000 | tf_op jit(solution)/shard_map/project_tokens/pallas_call | solution.py:202
  35.5 1.3 %all-to-all-done.1.parts_ref = bf16[32,2,576]{2,1,0:T(2,128)(2,1)S(1)} async-done(((bf16[32,2,576]{2,1,0:T(2,128)(2,1)}), bf16[32,2,576]{2,1,0:T(2,128)(2,1)S(1)}, u32[]{:S(2)}, u32[]{:S(2)}) %all-to-all-start.1) | async-done | bytes 73760 | tf_op jit(solution)/shard_map/spread_prefix/all_to_all | solution.py:197
  36.8 5.4 %key_grads.1 = (bf16[16,16,576]{2,1,0:T(8,128)(2,1)}, bf16[16,16,576]{2,1,0:T(8,128)(2,1)}, bf16[4,448,384]{2,1,0:T(8,128)(2,1)}, bf16[4,448,192]{2,1,0:T(8,128)(2,1)}) custom-call(bf16[32,2,576]{2,1,0:T(2,128)(2,1)S(1)} %all-to-all-done.1.parts_ref, bf16[2944,512]{1,0:T(8,128)(2,1)S(1)} %project_tokens.1.held_ref), custom_call_target="tpu_custom_call" | custom-call | flops 1000000000 | bytes 5000000 | tf_op jit(solution)/shard_map/key_grads/pallas_call | solution.py:217
  42.2 2.0 %collective-permute-start = (bf16[16,16,576]{2,1,0:T(8,128)(2,1)}, bf16[16,16,576]{2,1,0:T(8,128)(2,1)S(1)}, u32[]{:S(2)}, u32[]{:S(2)}) collective-permute-start(bf16[16,16,576]{2,1,0:T(8,128)(2,1)} %get-tuple-element.15), channel_id=1, source_target_pairs={{0,1},{1,0},{2,3},{3,2},{4,5},{5,4},{6,7},{7,6},{8,9},{9,8},{10,11... | collective-permute-start | bytes 884744 | tf_op jit(solution)/shard_map/sum_heads/ppermute | solution.py:241
  44.2 1.7 %collective-permute-done = bf16[16,16,576]{2,1,0:T(8,128)(2,1)S(1)} collective-permute-done((bf16[16,16,576]{2,1,0:T(8,128)(2,1)}, bf16[16,16,576]{2,1,0:T(8,128)(2,1)S(1)}, u32[]{:S(2)}, u32[]{:S(2)}) %collective-permute-start) | collective-permute-done | bytes 294944 | tf_op jit(solution)/shard_map/sum_heads/ppermute | solution.py:241
  45.9 1.8 %add_convert_fusion = bf16[16,16,576]{2,1,0:T(8,128)(2,1)} fusion(bf16[16,16,576]{2,1,0:T(8,128)(2,1)S(1)} %collective-permute-done, bf16[16,16,576]{2,1,0:T(8,128)(2,1)} %get-tuple-element.14), kind=kLoop, calls=%fused_computation.1 | loop fusion | flops 589824 | bytes 884736 | tf_op jit(solution)/shard_map/sum_heads/convert_element_type | solution.py:242
  47.7 5.5 %all-to-all-start.2 = ((bf16[16,16,576]{2,1,0:T(8,128)(2,1)}), bf16[16,16,576]{2,1,0:T(8,128)(2,1)S(1)}, u32[]{:S(2)}, u32[]{:S(2)}) async-start(bf16[16,16,576]{2,1,0:T(8,128)(2,1)} %add_convert_fusion), calls=%async_computation.2 | async-start | bytes 655360 | tf_op jit(solution)/shard_map/sum_heads/all_to_all | solution.py:244
  53.2 0.1 slice.17
  53.3 0.1 add_compare_fusion
  53.3 4.1 %query_grads.1 = bf16[4,192,384]{2,1,0:T(8,128)(2,1)} custom-call(bf16[4,448,192]{2,1,0:T(8,128)(2,1)} %get-tuple-element.16.key_ref, bf16[4,448,384]{2,1,0:T(8,128)(2,1)} %get-tuple-element.17.ds_ref), custom_call_target="tpu_custom_call" | custom-call | flops 320000000 | bytes 3000000 | tf_op jit(solution)/shard_map/query_grads/pallas_call | solution.py:247
  57.4 5.9 %all-to-all-done.2 = bf16[16,16,576]{2,1,0:T(8,128)(2,1)S(1)} async-done(((bf16[16,16,576]{2,1,0:T(8,128)(2,1)}), bf16[16,16,576]{2,1,0:T(8,128)(2,1)S(1)}, u32[]{:S(2)}, u32[]{:S(2)}) %all-to-all-start.2) | async-done | bytes 294944 | tf_op jit(solution)/shard_map/sum_heads/all_to_all | solution.py:244
  63.4 0.1 reduce
  63.5 0.6 broadcast_in_dim.45
  64.1 15.7 %all-to-all-start.3 = ((bf16[16,2,576]{2,1,0:T(2,128)(2,1)}), bf16[16,2,576]{2,1,0:T(2,128)(2,1)S(1)}, u32[]{:S(2)}, u32[]{:S(2)}) async-start(bf16[16,2,576]{2,1,0:T(2,128)(2,1)} %broadcast_in_dim.45), calls=%async_computation.3 | async-start | bytes 81920 | tf_op jit(solution)/shard_map/sum_slots/all_to_all | solution.py:263
  79.8 0.6 slice.23
  80.4 2.0 %all-to-all-done.3 = bf16[16,2,576]{2,1,0:T(2,128)(2,1)S(1)} async-done(((bf16[16,2,576]{2,1,0:T(2,128)(2,1)}), bf16[16,2,576]{2,1,0:T(2,128)(2,1)S(1)}, u32[]{:S(2)}, u32[]{:S(2)}) %all-to-all-start.3) | async-done | bytes 36896 | tf_op jit(solution)/shard_map/sum_slots/all_to_all | solution.py:263
  82.4 0.7 select_reduce_fusion
  (3 shorter events, 0.0 us)
Async XLA Ops:
  0.6 22.9 %copy-start = (s32[16]{0:T(128)S(1)}, s32[16]{0:T(128)}, u32[]{:S(2)}) copy-start(s32[16]{0:T(128)} %param.15) | copy-start | bytes 196
  2.0 23.4 %all-to-all-start = ((bf16[16,2,576]{2,1,0:T(2,128)(2,1)}), bf16[16,2,576]{2,1,0:T(2,128)(2,1)S(1)}, u32[]{:S(2)}, u32[]{:S(2)}) async-start(bf16[16,2,576]{2,1,0:T(2,128)(2,1)} %broadcast_in_dim.40), calls=%async_computation | async-start | bytes 81920 | tf_op jit(solution)/shard_map/fetch_slots/all_to_all | solution.py:190
  26.1 10.7 %all-to-all-start.1 = ((bf16[32,2,576]{2,1,0:T(2,128)(2,1)}), bf16[32,2,576]{2,1,0:T(2,128)(2,1)S(1)}, u32[]{:S(2)}, u32[]{:S(2)}) async-start(bf16[32,2,576]{2,1,0:T(2,128)(2,1)} %broadcast_in_dim.43), calls=%async_computation.1 | async-start | bytes 163840 | tf_op jit(solution)/shard_map/spread_prefix/all_to_all | solution.py:197
  42.2 3.7 %collective-permute-start = (bf16[16,16,576]{2,1,0:T(8,128)(2,1)}, bf16[16,16,576]{2,1,0:T(8,128)(2,1)S(1)}, u32[]{:S(2)}, u32[]{:S(2)}) collective-permute-start(bf16[16,16,576]{2,1,0:T(8,128)(2,1)} %get-tuple-element.15), channel_id=1, source_target_pairs={{0,1},{1,0},{2,3},{3,2},{4,5},{5,4},{6,7},{7,6},{8,9},{9,8},{10,11... | collective-permute-start | bytes 884744 | tf_op jit(solution)/shard_map/sum_heads/ppermute | solution.py:241
  47.7 15.7 %all-to-all-start.2 = ((bf16[16,16,576]{2,1,0:T(8,128)(2,1)}), bf16[16,16,576]{2,1,0:T(8,128)(2,1)S(1)}, u32[]{:S(2)}, u32[]{:S(2)}) async-start(bf16[16,16,576]{2,1,0:T(8,128)(2,1)} %add_convert_fusion), calls=%async_computation.2 | async-start | bytes 655360 | tf_op jit(solution)/shard_map/sum_heads/all_to_all | solution.py:244
  64.1 18.3 %all-to-all-start.3 = ((bf16[16,2,576]{2,1,0:T(2,128)(2,1)}), bf16[16,2,576]{2,1,0:T(2,128)(2,1)S(1)}, u32[]{:S(2)}, u32[]{:S(2)}) async-start(bf16[16,2,576]{2,1,0:T(2,128)(2,1)} %broadcast_in_dim.45), calls=%async_computation.3 | async-start | bytes 81920 | tf_op jit(solution)/shard_map/sum_slots/all_to_all | solution.py:263

commit v5 on v4

--- a/solution.py
+++ b/solution.py
@@ -15,6 +15,7 @@
 BLOCK = 128
 REQ_FIRST = 10
 HEAD_FIRST = 20
+SPREAD_FIRST = 20
 ANYWHERE = pl.BlockSpec(memory_space=pl.ANY)
 IN_VMEM = pl.BlockSpec(memory_space=pltpu.VMEM)
 PARAMS = pltpu.CompilerParams(vmem_limit_bytes=24 * 1024 * 1024)
@@ -145,6 +146,10 @@
         copy.wait()
 
 
+def add_shares(own_ref, given_ref, out_ref):
+    out_ref[...] = (own_ref[...].astype(f32) + given_ref[...].astype(f32)).astype(bf16)
+
+
 def query_grads(key_ref, ds_ref, out_ref):
     out_ref[...] = dot_tn(key_ref[...], ds_ref[...]).astype(bf16)
 
@@ -175,6 +180,7 @@
     req_first = REQ_FIRST % reqs
     req_group = from_first(req_first, reqs)
     head_group = from_first(HEAD_FIRST % heads, heads)
+    spread_group = from_first(SPREAD_FIRST % heads, heads)
     req_place = lax.axis_index("req")
     slot_ids = slot_of_tenant.at[tenant_of_request].get(mode="promise_in_bounds")
     my_slot = lax.dynamic_slice(slot_ids, (req_place,), (1,), allow_negative_indices=False)[0]
@@ -194,7 +200,7 @@
         place = lax.rem(my_slot + (reqs - req_first), reqs)
         rows = lax.dynamic_slice(all_slots, (place, 0, 0), (1, pre, lat), allow_negative_indices=False).astype(bf16)
         rows, d_out = lax.optimization_barrier((rows, d_out))
-        prefix = lax.all_to_all(jnp.broadcast_to(rows, (heads, pre, lat)), "head", 0, 0, axis_index_groups=head_group)
+        prefix = lax.all_to_all(jnp.broadcast_to(rows, (heads, pre, lat)), "head", 0, 0, axis_index_groups=spread_group)
 
     with jax.named_scope("project_tokens"):
         n_rows = max(x.stop for x in rows_held(n_h, seq).values())
@@ -219,7 +225,7 @@
             in_specs=[IN_VMEM] * 2,
             out_specs=[IN_VMEM, IN_VMEM, ANYWHERE, ANYWHERE],
             out_shape=[
-                pltpu.HBM((heads // 2, CHUNK, lat), bf16),
+                pltpu.VMEM((heads // 2, CHUNK, lat), bf16),
                 pltpu.HBM((heads // 2, CHUNK, lat), bf16),
                 pltpu.HBM((n_h, n_pre + seq, seq), bf16),
                 pltpu.HBM((n_h, n_pre + seq, d_q), bf16),
@@ -239,7 +245,14 @@
 
     with jax.named_scope("sum_heads"):
         given = lax.ppermute(other, "head", [(i, i ^ 1) for i in range(heads)])
-        summed = (own.astype(f32) + given.astype(f32)).astype(bf16)
+        summed = pl.pallas_call(
+            add_shares,
+            in_specs=[IN_VMEM] * 2,
+            out_specs=IN_VMEM,
+            out_shape=pltpu.HBM(own.shape, bf16),
+            compiler_params=PARAMS,
+            cost_estimate=cost(2e5, 1e6),
+        )(*keep(pltpu.VMEM, own), given)
         core_groups = [[i + core for i in head_group[0][::2]] for core in range(2)]
         parts = lax.all_to_all(summed, "head", 0, 0, axis_index_groups=core_groups)
 

time: 83.7 us -> 82.1 us (0.981)
  other arithmetic: 3.3 us -> 1.51 us
    convert_element_type x1 -> x0, other arithmetic: 1.79 us -> none  [shards(): summed = (own.astype(f32) + given.astype(f32)).astype(bf16)]
  transfers between devices with their start and end apart: 5 -> 5, of which waited for: 4 -> 4; matrix products, arithmetic and copies ran while one was open for 5% -> 6% of each run, Pallas kernels for 8% -> 8%
where the time goes in v5:
time: 82.1 us; the launch traced here: 81.5 us
  starting transfers between devices  49.3 us (60%)
  Pallas kernels  12 us (15%)
  waiting for transfers between devices  10.9 us (13%)
  local copies, waits for them, and re-layouts  6.41 us (8%)
  other arithmetic  1.51 us (2%)
  between operations  1.35 us (2%)
    all_to_all x1, starting transfers between devices, shards(): all_slots = lax.all_to_all(mine, 'req', 0, 0, axis_index_groups=req_group)  20.8 us
    all_to_all x1, starting transfers between devices, shards(): given = lax.all_to_all(sent, 'req', 0, 0, axis_index_groups=req_group)  15.7 us
    all_to_all x1, waiting for transfers between devices, shards(): parts = lax.all_to_all(summed, 'head', 0, 0, axis_index_groups=core_groups)  5.93 us
    all_to_all x1, starting transfers between devices, shards(): parts = lax.all_to_all(summed, 'head', 0, 0, axis_index_groups=core_groups)  5.46 us
    all_to_all x1, starting transfers between devices, shards(): lax.all_to_all(jnp.broadcast_to(rows, (heads, pre, lat)), 'head', 0, 0, a...  5.36 us
    pallas_call x1, Pallas kernels, shards(): pl.pallas_call(key_grads, in_specs=[IN_VMEM] * 2, out_specs=[IN_VMEM, IN_...  4.83 us
    pallas_call x1, Pallas kernels, shards(): pl.pallas_call(query_grads, grid=(n_h,), in_specs=[per_head(n_pre + seq,...  4.11 us
    pallas_call x1, Pallas kernels, shards(): pl.pallas_call(project_tokens, in_specs=[ANYWHERE] * 5, out_specs=IN_VMEM...  2.24 us
  transfers between devices with their start and end apart: 5, of which 4 were waited for; matrix products, arithmetic and copies ran while one was open for 6% of the time, Pallas kernels for 8%

profile of v5, /device:TPU:6, one launch (start us, length us, event | category | flops | bytes accessed | tf_op | source)
XLA Modules:
  0.0 81.5 jit_solution(8490270521069325811)
XLA Ops:
  0.6 0.0 copy-start
  0.6 1.3 %broadcast_in_dim.40 = bf16[16,2,576]{2,1,0:T(2,128)(2,1)} broadcast(f32[2,576]{1,0:T(2,128)} %bitcast.23), dimensions={1,2} | broadcast | bytes 41472 | tf_op jit(solution)/shard_map/fetch_slots/broadcast_in_dim | solution.py:195
  2.0 20.8 %all-to-all-start = ((bf16[16,2,576]{2,1,0:T(2,128)(2,1)}), bf16[16,2,576]{2,1,0:T(2,128)(2,1)S(1)}, u32[]{:S(2)}, u32[]{:S(2)}) async-start(bf16[16,2,576]{2,1,0:T(2,128)(2,1)} %broadcast_in_dim.40), calls=%async_computation | async-start | bytes 81920 | tf_op jit(solution)/shard_map/fetch_slots/all_to_all | solution.py:196
  22.8 0.7 compare_select_fusion
  23.5 0.0 copy-done
  23.5 0.7 gather_fusion
  24.1 0.6 dynamic_slice.6
  25.4 0.0 all-to-all-done
  25.4 0.7 broadcast_in_dim.43
  26.1 5.4 %all-to-all-start.1 = ((bf16[32,2,576]{2,1,0:T(2,128)(2,1)}), bf16[32,2,576]{2,1,0:T(2,128)(2,1)S(1)}, u32[]{:S(2)}, u32[]{:S(2)}) async-start(bf16[32,2,576]{2,1,0:T(2,128)(2,1)} %broadcast_in_dim.43), calls=%async_computation.1 | async-start | bytes 163840 | tf_op jit(solution)/shard_map/spread_prefix/all_to_all | solution.py:203
  31.5 1.8 %copy.15 = bf16[48,8,4,128]{3,1,2,0:T(8,128)(2,1)} copy(bf16[48,8,4,128]{3,2,1,0:T(4,128)(2,1)} %bitcast.20) | data formatting | bytes 786432
  33.3 2.2 %project_tokens.1.held_ref = bf16[2944,512]{1,0:T(8,128)(2,1)S(1)} custom-call(bf16[768,384]{1,0:T(8,128)(2,1)} %bitcast.16, bf16[384,512]{1,0:T(8,128)(2,1)} %bitcast.15, bf16[576,384]{1,0:T(8,128)(2,1)} %bitcast.19, bf16[512,512]{1,0:T(8,128)(2,1)} %bitcast.18, bf16[4,512,128]{2,1,0:T(8,128)(2,1)} %uv_hbm.1), custom_call_target="tpu_custom_call" | custom-call | flops 400000000 | bytes 5000000 | tf_op jit(solution)/shard_map/project_tokens/pallas_call | solution.py:208
  35.5 1.3 %all-to-all-done.1.parts_ref = bf16[32,2,576]{2,1,0:T(2,128)(2,1)S(1)} async-done(((bf16[32,2,576]{2,1,0:T(2,128)(2,1)}), bf16[32,2,576]{2,1,0:T(2,128)(2,1)S(1)}, u32[]{:S(2)}, u32[]{:S(2)}) %all-to-all-start.1) | async-done | bytes 73760 | tf_op jit(solution)/shard_map/spread_prefix/all_to_all | solution.py:203
  36.8 4.8 %key_grads.1 = (bf16[16,16,576]{2,1,0:T(8,128)(2,1)S(1)}, bf16[16,16,576]{2,1,0:T(8,128)(2,1)}, bf16[4,448,384]{2,1,0:T(8,128)(2,1)}, bf16[4,448,192]{2,1,0:T(8,128)(2,1)}) custom-call(bf16[32,2,576]{2,1,0:T(2,128)(2,1)S(1)} %all-to-all-done.1.parts_ref, bf16[2944,512]{1,0:T(8,128)(2,1)S(1)} %project_tokens.1.held_ref), custom_call_target="tpu_custom_call" | custom-call | flops 1000000000 | bytes 5000000 | tf_op jit(solution)/shard_map/key_grads/pallas_call | solution.py:223
  41.6 2.0 %collective-permute-start = (bf16[16,16,576]{2,1,0:T(8,128)(2,1)}, bf16[16,16,576]{2,1,0:T(8,128)(2,1)S(1)}, u32[]{:S(2)}, u32[]{:S(2)}) collective-permute-start(bf16[16,16,576]{2,1,0:T(8,128)(2,1)} %get-tuple-element.15), channel_id=1, source_target_pairs={{0,1},{1,0},{2,3},{3,2},{4,5},{5,4},{6,7},{7,6},{8,9},{9,8},{10,11... | collective-permute-start | bytes 884744 | tf_op jit(solution)/shard_map/sum_heads/ppermute | solution.py:247
  43.7 1.7 %collective-permute-done.given_ref = bf16[16,16,576]{2,1,0:T(8,128)(2,1)S(1)} collective-permute-done((bf16[16,16,576]{2,1,0:T(8,128)(2,1)}, bf16[16,16,576]{2,1,0:T(8,128)(2,1)S(1)}, u32[]{:S(2)}, u32[]{:S(2)}) %collective-permute-start) | collective-permute-done | bytes 294944 | tf_op jit(solution)/shard_map/sum_heads/ppermute | solution.py:247
  45.4 0.8 sum_heads.1
  46.2 5.5 %all-to-all-start.2 = ((bf16[16,16,576]{2,1,0:T(8,128)(2,1)}), bf16[16,16,576]{2,1,0:T(8,128)(2,1)S(1)}, u32[]{:S(2)}, u32[]{:S(2)}) async-start(bf16[16,16,576]{2,1,0:T(8,128)(2,1)} %sum_heads.1), calls=%async_computation.2 | async-start | bytes 655360 | tf_op jit(solution)/shard_map/sum_heads/all_to_all | solution.py:257
  51.6 0.1 slice.17
  51.7 0.1 add_compare_fusion
  51.8 4.1 %query_grads.1 = bf16[4,192,384]{2,1,0:T(8,128)(2,1)} custom-call(bf16[4,448,192]{2,1,0:T(8,128)(2,1)} %get-tuple-element.16.key_ref, bf16[4,448,384]{2,1,0:T(8,128)(2,1)} %get-tuple-element.17.ds_ref), custom_call_target="tpu_custom_call" | custom-call | flops 320000000 | bytes 3000000 | tf_op jit(solution)/shard_map/query_grads/pallas_call | solution.py:260
  55.9 5.9 %all-to-all-done.2 = bf16[16,16,576]{2,1,0:T(8,128)(2,1)S(1)} async-done(((bf16[16,16,576]{2,1,0:T(8,128)(2,1)}), bf16[16,16,576]{2,1,0:T(8,128)(2,1)S(1)}, u32[]{:S(2)}, u32[]{:S(2)}) %all-to-all-start.2) | async-done | bytes 294944 | tf_op jit(solution)/shard_map/sum_heads/all_to_all | solution.py:257
  61.8 0.1 reduce
  61.9 0.6 broadcast_in_dim.45
  62.5 15.7 %all-to-all-start.3 = ((bf16[16,2,576]{2,1,0:T(2,128)(2,1)}), bf16[16,2,576]{2,1,0:T(2,128)(2,1)S(1)}, u32[]{:S(2)}, u32[]{:S(2)}) async-start(bf16[16,2,576]{2,1,0:T(2,128)(2,1)} %broadcast_in_dim.45), calls=%async_computation.3 | async-start | bytes 81920 | tf_op jit(solution)/shard_map/sum_slots/all_to_all | solution.py:276
  78.2 0.6 slice.23
  78.8 2.0 %all-to-all-done.3 = bf16[16,2,576]{2,1,0:T(2,128)(2,1)S(1)} async-done(((bf16[16,2,576]{2,1,0:T(2,128)(2,1)}), bf16[16,2,576]{2,1,0:T(2,128)(2,1)S(1)}, u32[]{:S(2)}, u32[]{:S(2)}) %all-to-all-start.3) | async-done | bytes 36896 | tf_op jit(solution)/shard_map/sum_slots/all_to_all | solution.py:276
  80.8 0.7 select_reduce_fusion
  (3 shorter events, 0.0 us)
Async XLA Ops:
  0.6 22.9 %copy-start = (s32[16]{0:T(128)S(1)}, s32[16]{0:T(128)}, u32[]{:S(2)}) copy-start(s32[16]{0:T(128)} %param.15) | copy-start | bytes 196
  2.0 23.4 %all-to-all-start = ((bf16[16,2,576]{2,1,0:T(2,128)(2,1)}), bf16[16,2,576]{2,1,0:T(2,128)(2,1)S(1)}, u32[]{:S(2)}, u32[]{:S(2)}) async-start(bf16[16,2,576]{2,1,0:T(2,128)(2,1)} %broadcast_in_dim.40), calls=%async_computation | async-start | bytes 81920 | tf_op jit(solution)/shard_map/fetch_slots/all_to_all | solution.py:196
  26.1 10.7 %all-to-all-start.1 = ((bf16[32,2,576]{2,1,0:T(2,128)(2,1)}), bf16[32,2,576]{2,1,0:T(2,128)(2,1)S(1)}, u32[]{:S(2)}, u32[]{:S(2)}) async-start(bf16[32,2,576]{2,1,0:T(2,128)(2,1)} %broadcast_in_dim.43), calls=%async_computation.1 | async-start | bytes 163840 | tf_op jit(solution)/shard_map/spread_prefix/all_to_all | solution.py:203
  41.6 3.7 %collective-permute-start = (bf16[16,16,576]{2,1,0:T(8,128)(2,1)}, bf16[16,16,576]{2,1,0:T(8,128)(2,1)S(1)}, u32[]{:S(2)}, u32[]{:S(2)}) collective-permute-start(bf16[16,16,576]{2,1,0:T(8,128)(2,1)} %get-tuple-element.15), channel_id=1, source_target_pairs={{0,1},{1,0},{2,3},{3,2},{4,5},{5,4},{6,7},{7,6},{8,9},{9,8},{10,11... | collective-permute-start | bytes 884744 | tf_op jit(solution)/shard_map/sum_heads/ppermute | solution.py:247
  46.2 15.7 %all-to-all-start.2 = ((bf16[16,16,576]{2,1,0:T(8,128)(2,1)}), bf16[16,16,576]{2,1,0:T(8,128)(2,1)S(1)}, u32[]{:S(2)}, u32[]{:S(2)}) async-start(bf16[16,16,576]{2,1,0:T(8,128)(2,1)} %sum_heads.1), calls=%async_computation.2 | async-start | bytes 655360 | tf_op jit(solution)/shard_map/sum_heads/all_to_all | solution.py:257
  62.5 18.3 %all-to-all-start.3 = ((bf16[16,2,576]{2,1,0:T(2,128)(2,1)}), bf16[16,2,576]{2,1,0:T(2,128)(2,1)S(1)}, u32[]{:S(2)}, u32[]{:S(2)}) async-start(bf16[16,2,576]{2,1,0:T(2,128)(2,1)} %broadcast_in_dim.45), calls=%async_computation.3 | async-start | bytes 81920 | tf_op jit(solution)/shard_map/sum_slots/all_to_all | solution.py:276

commit v6 on v5

--- a/solution.py
+++ b/solution.py
@@ -226,7 +226,7 @@
             out_specs=[IN_VMEM, IN_VMEM, ANYWHERE, ANYWHERE],
             out_shape=[
                 pltpu.VMEM((heads // 2, CHUNK, lat), bf16),
-                pltpu.HBM((heads // 2, CHUNK, lat), bf16),
+                pltpu.VMEM((heads // 2, CHUNK, lat), bf16),
                 pltpu.HBM((n_h, n_pre + seq, seq), bf16),
                 pltpu.HBM((n_h, n_pre + seq, d_q), bf16),
             ],

time: 82.1 us -> 81.3 us (level)
  no operation moved by 1% of the time
where the time goes in v6:
time: 81.3 us; the launch traced here: 80.7 us
  starting transfers between devices  49.3 us (61%)
  Pallas kernels  11.4 us (14%)
  waiting for transfers between devices  10.7 us (13%)
  local copies, waits for them, and re-layouts  6.41 us (8%)
  other arithmetic  1.51 us (2%)
  between operations  1.35 us (2%)
    all_to_all x1, starting transfers between devices, shards(): all_slots = lax.all_to_all(mine, 'req', 0, 0, axis_index_groups=req_group)  20.8 us
    all_to_all x1, starting transfers between devices, shards(): given = lax.all_to_all(sent, 'req', 0, 0, axis_index_groups=req_group)  15.7 us
    all_to_all x1, waiting for transfers between devices, shards(): parts = lax.all_to_all(summed, 'head', 0, 0, axis_index_groups=core_groups)  5.94 us
    all_to_all x1, starting transfers between devices, shards(): parts = lax.all_to_all(summed, 'head', 0, 0, axis_index_groups=core_groups)  5.47 us
    all_to_all x1, starting transfers between devices, shards(): lax.all_to_all(jnp.broadcast_to(rows, (heads, pre, lat)), 'head', 0, 0, a...  5.36 us
    pallas_call x1, Pallas kernels, shards(): pl.pallas_call(key_grads, in_specs=[IN_VMEM] * 2, out_specs=[IN_VMEM, IN_...  4.22 us
    pallas_call x1, Pallas kernels, shards(): pl.pallas_call(query_grads, grid=(n_h,), in_specs=[per_head(n_pre + seq,...  4.1 us
    pallas_call x1, Pallas kernels, shards(): pl.pallas_call(project_tokens, in_specs=[ANYWHERE] * 5, out_specs=IN_VMEM...  2.24 us
  transfers between devices with their start and end apart: 5, of which 4 were waited for; matrix products, arithmetic and copies ran while one was open for 6% of the time, Pallas kernels for 8%

profile of v6, /device:TPU:6, one launch (start us, length us, event | category | flops | bytes accessed | tf_op | source)
XLA Modules:
  0.0 80.7 jit_solution(18046785438218183577)
XLA Ops:
  0.6 0.0 copy-start
  0.6 1.3 %broadcast_in_dim.40 = bf16[16,2,576]{2,1,0:T(2,128)(2,1)} broadcast(f32[2,576]{1,0:T(2,128)} %bitcast.23), dimensions={1,2} | broadcast | bytes 41472 | tf_op jit(solution)/shard_map/fetch_slots/broadcast_in_dim | solution.py:195
  2.0 20.8 %all-to-all-start = ((bf16[16,2,576]{2,1,0:T(2,128)(2,1)}), bf16[16,2,576]{2,1,0:T(2,128)(2,1)S(1)}, u32[]{:S(2)}, u32[]{:S(2)}) async-start(bf16[16,2,576]{2,1,0:T(2,128)(2,1)} %broadcast_in_dim.40), calls=%async_computation | async-start | bytes 81920 | tf_op jit(solution)/shard_map/fetch_slots/all_to_all | solution.py:196
  22.8 0.7 compare_select_fusion
  23.5 0.0 copy-done
  23.5 0.7 gather_fusion
  24.1 0.6 dynamic_slice.6
  25.4 0.0 all-to-all-done
  25.4 0.7 broadcast_in_dim.43
  26.1 5.4 %all-to-all-start.1 = ((bf16[32,2,576]{2,1,0:T(2,128)(2,1)}), bf16[32,2,576]{2,1,0:T(2,128)(2,1)S(1)}, u32[]{:S(2)}, u32[]{:S(2)}) async-start(bf16[32,2,576]{2,1,0:T(2,128)(2,1)} %broadcast_in_dim.43), calls=%async_computation.1 | async-start | bytes 163840 | tf_op jit(solution)/shard_map/spread_prefix/all_to_all | solution.py:203
  31.5 1.8 %copy.15 = bf16[48,8,4,128]{3,1,2,0:T(8,128)(2,1)} copy(bf16[48,8,4,128]{3,2,1,0:T(4,128)(2,1)} %bitcast.20) | data formatting | bytes 786432
  33.3 2.2 %project_tokens.1.held_ref = bf16[2944,512]{1,0:T(8,128)(2,1)S(1)} custom-call(bf16[768,384]{1,0:T(8,128)(2,1)} %bitcast.16, bf16[384,512]{1,0:T(8,128)(2,1)} %bitcast.15, bf16[576,384]{1,0:T(8,128)(2,1)} %bitcast.19, bf16[512,512]{1,0:T(8,128)(2,1)} %bitcast.18, bf16[4,512,128]{2,1,0:T(8,128)(2,1)} %uv_hbm.1), custom_call_target="tpu_custom_call" | custom-call | flops 400000000 | bytes 5000000 | tf_op jit(solution)/shard_map/project_tokens/pallas_call | solution.py:208
  35.5 1.3 %all-to-all-done.1.parts_ref = bf16[32,2,576]{2,1,0:T(2,128)(2,1)S(1)} async-done(((bf16[32,2,576]{2,1,0:T(2,128)(2,1)}), bf16[32,2,576]{2,1,0:T(2,128)(2,1)S(1)}, u32[]{:S(2)}, u32[]{:S(2)}) %all-to-all-start.1) | async-done | bytes 73760 | tf_op jit(solution)/shard_map/spread_prefix/all_to_all | solution.py:203
  36.8 4.2 %key_grads.1 = (bf16[16,16,576]{2,1,0:T(8,128)(2,1)S(1)}, bf16[16,16,576]{2,1,0:T(8,128)(2,1)S(1)}, bf16[4,448,384]{2,1,0:T(8,128)(2,1)}, bf16[4,448,192]{2,1,0:T(8,128)(2,1)}) custom-call(bf16[32,2,576]{2,1,0:T(2,128)(2,1)S(1)} %all-to-all-done.1.parts_ref, bf16[2944,512]{1,0:T(8,128)(2,1)S(1)} %project_tokens.1.held_ref), custom_call_target="tpu_custom_call" | custom-call | flops 1000000000 | bytes 5000000 | tf_op jit(solution)/shard_map/key_grads/pallas_call | solution.py:223
  41.0 2.0 %collective-permute-start = (bf16[16,16,576]{2,1,0:T(8,128)(2,1)S(1)}, bf16[16,16,576]{2,1,0:T(8,128)(2,1)S(1)}, u32[]{:S(2)}, u32[]{:S(2)}) collective-permute-start(bf16[16,16,576]{2,1,0:T(8,128)(2,1)S(1)} %get-tuple-element.15), channel_id=1, source_target_pairs={{0,1},{1,0},{2,3},{3,2},{4,5},{5,4},{6,7},{7,6},{8,9},{9,8},{10,11... | collective-permute-start | bytes 884744 | tf_op jit(solution)/shard_map/sum_heads/ppermute | solution.py:247
  43.1 1.5 %collective-permute-done.given_ref = bf16[16,16,576]{2,1,0:T(8,128)(2,1)S(1)} collective-permute-done((bf16[16,16,576]{2,1,0:T(8,128)(2,1)S(1)}, bf16[16,16,576]{2,1,0:T(8,128)(2,1)S(1)}, u32[]{:S(2)}, u32[]{:S(2)}) %collective-permute-start) | collective-permute-done | bytes 294944 | tf_op jit(solution)/shard_map/sum_heads/ppermute | solution.py:247
  44.5 0.8 %sum_heads.1 = bf16[16,16,576]{2,1,0:T(8,128)(2,1)} custom-call(bf16[16,16,576]{2,1,0:T(8,128)(2,1)S(1)} %get-tuple-element.14.own_ref, bf16[16,16,576]{2,1,0:T(8,128)(2,1)S(1)} %collective-permute-done.given_ref), custom_call_target="tpu_custom_call" | custom-call | flops 200000 | bytes 1000000 | tf_op jit(solution)/shard_map/sum_heads/pallas_call | solution.py:248
  45.4 5.5 %all-to-all-start.2 = ((bf16[16,16,576]{2,1,0:T(8,128)(2,1)}), bf16[16,16,576]{2,1,0:T(8,128)(2,1)S(1)}, u32[]{:S(2)}, u32[]{:S(2)}) async-start(bf16[16,16,576]{2,1,0:T(8,128)(2,1)} %sum_heads.1), calls=%async_computation.2 | async-start | bytes 655360 | tf_op jit(solution)/shard_map/sum_heads/all_to_all | solution.py:257
  50.8 0.1 slice.17
  50.9 0.1 add_compare_fusion
  51.0 4.1 %query_grads.1 = bf16[4,192,384]{2,1,0:T(8,128)(2,1)} custom-call(bf16[4,448,192]{2,1,0:T(8,128)(2,1)} %get-tuple-element.16.key_ref, bf16[4,448,384]{2,1,0:T(8,128)(2,1)} %get-tuple-element.17.ds_ref), custom_call_target="tpu_custom_call" | custom-call | flops 320000000 | bytes 3000000 | tf_op jit(solution)/shard_map/query_grads/pallas_call | solution.py:260
  55.1 5.9 %all-to-all-done.2 = bf16[16,16,576]{2,1,0:T(8,128)(2,1)S(1)} async-done(((bf16[16,16,576]{2,1,0:T(8,128)(2,1)}), bf16[16,16,576]{2,1,0:T(8,128)(2,1)S(1)}, u32[]{:S(2)}, u32[]{:S(2)}) %all-to-all-start.2) | async-done | bytes 294944 | tf_op jit(solution)/shard_map/sum_heads/all_to_all | solution.py:257
  61.0 0.1 reduce
  61.1 0.6 broadcast_in_dim.45
  61.7 15.7 %all-to-all-start.3 = ((bf16[16,2,576]{2,1,0:T(2,128)(2,1)}), bf16[16,2,576]{2,1,0:T(2,128)(2,1)S(1)}, u32[]{:S(2)}, u32[]{:S(2)}) async-start(bf16[16,2,576]{2,1,0:T(2,128)(2,1)} %broadcast_in_dim.45), calls=%async_computation.3 | async-start | bytes 81920 | tf_op jit(solution)/shard_map/sum_slots/all_to_all | solution.py:276
  77.4 0.6 slice.23
  78.0 2.0 %all-to-all-done.3 = bf16[16,2,576]{2,1,0:T(2,128)(2,1)S(1)} async-done(((bf16[16,2,576]{2,1,0:T(2,128)(2,1)}), bf16[16,2,576]{2,1,0:T(2,128)(2,1)S(1)}, u32[]{:S(2)}, u32[]{:S(2)}) %all-to-all-start.3) | async-done | bytes 36896 | tf_op jit(solution)/shard_map/sum_slots/all_to_all | solution.py:276
  80.0 0.7 select_reduce_fusion
  (3 shorter events, 0.0 us)
Async XLA Ops:
  0.6 22.9 %copy-start = (s32[16]{0:T(128)S(1)}, s32[16]{0:T(128)}, u32[]{:S(2)}) copy-start(s32[16]{0:T(128)} %param.15) | copy-start | bytes 196
  2.0 23.4 %all-to-all-start = ((bf16[16,2,576]{2,1,0:T(2,128)(2,1)}), bf16[16,2,576]{2,1,0:T(2,128)(2,1)S(1)}, u32[]{:S(2)}, u32[]{:S(2)}) async-start(bf16[16,2,576]{2,1,0:T(2,128)(2,1)} %broadcast_in_dim.40), calls=%async_computation | async-start | bytes 81920 | tf_op jit(solution)/shard_map/fetch_slots/all_to_all | solution.py:196
  26.1 10.7 %all-to-all-start.1 = ((bf16[32,2,576]{2,1,0:T(2,128)(2,1)}), bf16[32,2,576]{2,1,0:T(2,128)(2,1)S(1)}, u32[]{:S(2)}, u32[]{:S(2)}) async-start(bf16[32,2,576]{2,1,0:T(2,128)(2,1)} %broadcast_in_dim.43), calls=%async_computation.1 | async-start | bytes 163840 | tf_op jit(solution)/shard_map/spread_prefix/all_to_all | solution.py:203
  41.0 3.5 %collective-permute-start = (bf16[16,16,576]{2,1,0:T(8,128)(2,1)S(1)}, bf16[16,16,576]{2,1,0:T(8,128)(2,1)S(1)}, u32[]{:S(2)}, u32[]{:S(2)}) collective-permute-start(bf16[16,16,576]{2,1,0:T(8,128)(2,1)S(1)} %get-tuple-element.15), channel_id=1, source_target_pairs={{0,1},{1,0},{2,3},{3,2},{4,5},{5,4},{6,7},{7,6},{8,9},{9,8},{10,11... | collective-permute-start | bytes 884744 | tf_op jit(solution)/shard_map/sum_heads/ppermute | solution.py:247
  45.4 15.7 %all-to-all-start.2 = ((bf16[16,16,576]{2,1,0:T(8,128)(2,1)}), bf16[16,16,576]{2,1,0:T(8,128)(2,1)S(1)}, u32[]{:S(2)}, u32[]{:S(2)}) async-start(bf16[16,16,576]{2,1,0:T(8,128)(2,1)} %sum_heads.1), calls=%async_computation.2 | async-start | bytes 655360 | tf_op jit(solution)/shard_map/sum_heads/all_to_all | solution.py:257
  61.7 18.3 %all-to-all-start.3 = ((bf16[16,2,576]{2,1,0:T(2,128)(2,1)}), bf16[16,2,576]{2,1,0:T(2,128)(2,1)S(1)}, u32[]{:S(2)}, u32[]{:S(2)}) async-start(bf16[16,2,576]{2,1,0:T(2,128)(2,1)} %broadcast_in_dim.45), calls=%async_computation.3 | async-start | bytes 81920 | tf_op jit(solution)/shard_map/sum_slots/all_to_all | solution.py:276

commit v7 on v6

--- a/solution.py
+++ b/solution.py
@@ -113,14 +113,14 @@
             probs = terms * (1.0 / jnp.sum(terms, axis=0, keepdims=True))
             delta = jnp.sum(probs * d_probs, axis=0, keepdims=True)
             probs_ref[h, :seen, here] = probs.astype(bf16)
-            ds_ref[h, :seen, here] = (probs * (d_probs - delta) * SCALE).astype(bf16)
+            ds_ref[h, :seen, here] = (probs * (d_probs - delta)).astype(bf16)
             if seen < n_keys:
                 probs_ref[h, seen:, here] = jnp.zeros((n_keys - seen, BLOCK), bf16)
                 ds_ref[h, seen:, here] = jnp.zeros((n_keys - seen, BLOCK), bf16)
         for i, (kept, target) in enumerate(((key_ref, key_hbm), (ds_ref, ds_hbm))):
             out.append(pltpu.make_async_copy(kept.at[h], target.at[h], sems.at[h, i]))
             out[-1].start()
-        ds_q = dot_nt(ds_ref[h], held_ref[q_rows, :seq])
+        ds_q = dot_nt(ds_ref[h], held_ref[q_rows, :seq]) * SCALE
         key_sides.append(ds_q[:, :D_NOPE].astype(bf16))
         val_sides.append(dot(probs_ref[h], held_ref[rows["do"], mine]).astype(bf16))
         rope = ds_q[:, D_NOPE:] if rope is None else rope + ds_q[:, D_NOPE:]
@@ -151,7 +151,7 @@
 
 
 def query_grads(key_ref, ds_ref, out_ref):
-    out_ref[...] = dot_tn(key_ref[...], ds_ref[...]).astype(bf16)
+    out_ref[...] = (dot_tn(key_ref[...], ds_ref[...]) * SCALE).astype(bf16)
 
 
 def per_head(*shape):

time: 81.3 us -> 81.2 us (level)
  no operation moved by 1% of the time
where the time goes in v7:
time: 81.2 us; the launch traced here: 80.6 us
  starting transfers between devices  49.4 us (61%)
  Pallas kernels  11.3 us (14%)
  waiting for transfers between devices  10.7 us (13%)
  local copies, waits for them, and re-layouts  6.41 us (8%)
  other arithmetic  1.51 us (2%)
  between operations  1.35 us (2%)
    all_to_all x1, starting transfers between devices, shards(): all_slots = lax.all_to_all(mine, 'req', 0, 0, axis_index_groups=req_group)  20.8 us
    all_to_all x1, starting transfers between devices, shards(): given = lax.all_to_all(sent, 'req', 0, 0, axis_index_groups=req_group)  15.7 us
    all_to_all x1, waiting for transfers between devices, shards(): parts = lax.all_to_all(summed, 'head', 0, 0, axis_index_groups=core_groups)  5.94 us
    all_to_all x1, starting transfers between devices, shards(): parts = lax.all_to_all(summed, 'head', 0, 0, axis_index_groups=core_groups)  5.47 us
    all_to_all x1, starting transfers between devices, shards(): lax.all_to_all(jnp.broadcast_to(rows, (heads, pre, lat)), 'head', 0, 0, a...  5.36 us
    pallas_call x1, Pallas kernels, shards(): pl.pallas_call(key_grads, in_specs=[IN_VMEM] * 2, out_specs=[IN_VMEM, IN_...  4.14 us
    pallas_call x1, Pallas kernels, shards(): pl.pallas_call(query_grads, grid=(n_h,), in_specs=[per_head(n_pre + seq,...  4.1 us
    pallas_call x1, Pallas kernels, shards(): pl.pallas_call(project_tokens, in_specs=[ANYWHERE] * 5, out_specs=IN_VMEM...  2.24 us
  transfers between devices with their start and end apart: 5, of which 4 were waited for; matrix products, arithmetic and copies ran while one was open for 6% of the time, Pallas kernels for 8%

profile of v7, /device:TPU:6, one launch (start us, length us, event | category | flops | bytes accessed | tf_op | source)
XLA Modules:
  0.0 80.6 jit_solution(3736457575884123391)
XLA Ops:
  0.6 0.0 copy-start
  0.6 1.3 %broadcast_in_dim.40 = bf16[16,2,576]{2,1,0:T(2,128)(2,1)} broadcast(f32[2,576]{1,0:T(2,128)} %bitcast.23), dimensions={1,2} | broadcast | bytes 41472 | tf_op jit(solution)/shard_map/fetch_slots/broadcast_in_dim | solution.py:195
  2.0 20.8 %all-to-all-start = ((bf16[16,2,576]{2,1,0:T(2,128)(2,1)}), bf16[16,2,576]{2,1,0:T(2,128)(2,1)S(1)}, u32[]{:S(2)}, u32[]{:S(2)}) async-start(bf16[16,2,576]{2,1,0:T(2,128)(2,1)} %broadcast_in_dim.40), calls=%async_computation | async-start | bytes 81920 | tf_op jit(solution)/shard_map/fetch_slots/all_to_all | solution.py:196
  22.8 0.7 compare_select_fusion
  23.5 0.0 copy-done
  23.5 0.7 gather_fusion
  24.1 0.6 dynamic_slice.6
  25.4 0.0 all-to-all-done
  25.4 0.7 broadcast_in_dim.43
  26.1 5.4 %all-to-all-start.1 = ((bf16[32,2,576]{2,1,0:T(2,128)(2,1)}), bf16[32,2,576]{2,1,0:T(2,128)(2,1)S(1)}, u32[]{:S(2)}, u32[]{:S(2)}) async-start(bf16[32,2,576]{2,1,0:T(2,128)(2,1)} %broadcast_in_dim.43), calls=%async_computation.1 | async-start | bytes 163840 | tf_op jit(solution)/shard_map/spread_prefix/all_to_all | solution.py:203
  31.5 1.8 %copy.15 = bf16[48,8,4,128]{3,1,2,0:T(8,128)(2,1)} copy(bf16[48,8,4,128]{3,2,1,0:T(4,128)(2,1)} %bitcast.20) | data formatting | bytes 786432
  33.3 2.2 %project_tokens.1.held_ref = bf16[2944,512]{1,0:T(8,128)(2,1)S(1)} custom-call(bf16[768,384]{1,0:T(8,128)(2,1)} %bitcast.16, bf16[384,512]{1,0:T(8,128)(2,1)} %bitcast.15, bf16[576,384]{1,0:T(8,128)(2,1)} %bitcast.19, bf16[512,512]{1,0:T(8,128)(2,1)} %bitcast.18, bf16[4,512,128]{2,1,0:T(8,128)(2,1)} %uv_hbm.1), custom_call_target="tpu_custom_call" | custom-call | flops 400000000 | bytes 5000000 | tf_op jit(solution)/shard_map/project_tokens/pallas_call | solution.py:208
  35.5 1.3 %all-to-all-done.1.parts_ref = bf16[32,2,576]{2,1,0:T(2,128)(2,1)S(1)} async-done(((bf16[32,2,576]{2,1,0:T(2,128)(2,1)}), bf16[32,2,576]{2,1,0:T(2,128)(2,1)S(1)}, u32[]{:S(2)}, u32[]{:S(2)}) %all-to-all-start.1) | async-done | bytes 73760 | tf_op jit(solution)/shard_map/spread_prefix/all_to_all | solution.py:203
  36.8 4.1 %key_grads.1 = (bf16[16,16,576]{2,1,0:T(8,128)(2,1)S(1)}, bf16[16,16,576]{2,1,0:T(8,128)(2,1)S(1)}, bf16[4,448,384]{2,1,0:T(8,128)(2,1)}, bf16[4,448,192]{2,1,0:T(8,128)(2,1)}) custom-call(bf16[32,2,576]{2,1,0:T(2,128)(2,1)S(1)} %all-to-all-done.1.parts_ref, bf16[2944,512]{1,0:T(8,128)(2,1)S(1)} %project_tokens.1.held_ref), custom_call_target="tpu_custom_call" | custom-call | flops 1000000000 | bytes 5000000 | tf_op jit(solution)/shard_map/key_grads/pallas_call | solution.py:223
  40.9 2.0 %collective-permute-start = (bf16[16,16,576]{2,1,0:T(8,128)(2,1)S(1)}, bf16[16,16,576]{2,1,0:T(8,128)(2,1)S(1)}, u32[]{:S(2)}, u32[]{:S(2)}) collective-permute-start(bf16[16,16,576]{2,1,0:T(8,128)(2,1)S(1)} %get-tuple-element.15), channel_id=1, source_target_pairs={{0,1},{1,0},{2,3},{3,2},{4,5},{5,4},{6,7},{7,6},{8,9},{9,8},{10,11... | collective-permute-start | bytes 884744 | tf_op jit(solution)/shard_map/sum_heads/ppermute | solution.py:247
  43.0 1.5 %collective-permute-done.given_ref = bf16[16,16,576]{2,1,0:T(8,128)(2,1)S(1)} collective-permute-done((bf16[16,16,576]{2,1,0:T(8,128)(2,1)S(1)}, bf16[16,16,576]{2,1,0:T(8,128)(2,1)S(1)}, u32[]{:S(2)}, u32[]{:S(2)}) %collective-permute-start) | collective-permute-done | bytes 294944 | tf_op jit(solution)/shard_map/sum_heads/ppermute | solution.py:247
  44.5 0.8 %sum_heads.1 = bf16[16,16,576]{2,1,0:T(8,128)(2,1)} custom-call(bf16[16,16,576]{2,1,0:T(8,128)(2,1)S(1)} %get-tuple-element.14.own_ref, bf16[16,16,576]{2,1,0:T(8,128)(2,1)S(1)} %collective-permute-done.given_ref), custom_call_target="tpu_custom_call" | custom-call | flops 200000 | bytes 1000000 | tf_op jit(solution)/shard_map/sum_heads/pallas_call | solution.py:248
  45.3 5.5 %all-to-all-start.2 = ((bf16[16,16,576]{2,1,0:T(8,128)(2,1)}), bf16[16,16,576]{2,1,0:T(8,128)(2,1)S(1)}, u32[]{:S(2)}, u32[]{:S(2)}) async-start(bf16[16,16,576]{2,1,0:T(8,128)(2,1)} %sum_heads.1), calls=%async_computation.2 | async-start | bytes 655360 | tf_op jit(solution)/shard_map/sum_heads/all_to_all | solution.py:257
  50.7 0.1 slice.17
  50.8 0.1 add_compare_fusion
  50.9 4.1 %query_grads.1 = bf16[4,192,384]{2,1,0:T(8,128)(2,1)} custom-call(bf16[4,448,192]{2,1,0:T(8,128)(2,1)} %get-tuple-element.16.key_ref, bf16[4,448,384]{2,1,0:T(8,128)(2,1)} %get-tuple-element.17.ds_ref), custom_call_target="tpu_custom_call" | custom-call | flops 320000000 | bytes 3000000 | tf_op jit(solution)/shard_map/query_grads/pallas_call | solution.py:260
  55.0 5.9 %all-to-all-done.2 = bf16[16,16,576]{2,1,0:T(8,128)(2,1)S(1)} async-done(((bf16[16,16,576]{2,1,0:T(8,128)(2,1)}), bf16[16,16,576]{2,1,0:T(8,128)(2,1)S(1)}, u32[]{:S(2)}, u32[]{:S(2)}) %all-to-all-start.2) | async-done | bytes 294944 | tf_op jit(solution)/shard_map/sum_heads/all_to_all | solution.py:257
  60.9 0.1 reduce
  61.0 0.6 broadcast_in_dim.45
  61.7 15.7 %all-to-all-start.3 = ((bf16[16,2,576]{2,1,0:T(2,128)(2,1)}), bf16[16,2,576]{2,1,0:T(2,128)(2,1)S(1)}, u32[]{:S(2)}, u32[]{:S(2)}) async-start(bf16[16,2,576]{2,1,0:T(2,128)(2,1)} %broadcast_in_dim.45), calls=%async_computation.3 | async-start | bytes 81920 | tf_op jit(solution)/shard_map/sum_slots/all_to_all | solution.py:276
  77.3 0.6 slice.23
  77.9 2.0 %all-to-all-done.3 = bf16[16,2,576]{2,1,0:T(2,128)(2,1)S(1)} async-done(((bf16[16,2,576]{2,1,0:T(2,128)(2,1)}), bf16[16,2,576]{2,1,0:T(2,128)(2,1)S(1)}, u32[]{:S(2)}, u32[]{:S(2)}) %all-to-all-start.3) | async-done | bytes 36896 | tf_op jit(solution)/shard_map/sum_slots/all_to_all | solution.py:276
  79.9 0.7 select_reduce_fusion
  (3 shorter events, 0.0 us)
Async XLA Ops:
  0.6 22.9 %copy-start = (s32[16]{0:T(128)S(1)}, s32[16]{0:T(128)}, u32[]{:S(2)}) copy-start(s32[16]{0:T(128)} %param.15) | copy-start | bytes 196
  2.0 23.4 %all-to-all-start = ((bf16[16,2,576]{2,1,0:T(2,128)(2,1)}), bf16[16,2,576]{2,1,0:T(2,128)(2,1)S(1)}, u32[]{:S(2)}, u32[]{:S(2)}) async-start(bf16[16,2,576]{2,1,0:T(2,128)(2,1)} %broadcast_in_dim.40), calls=%async_computation | async-start | bytes 81920 | tf_op jit(solution)/shard_map/fetch_slots/all_to_all | solution.py:196
  26.1 10.7 %all-to-all-start.1 = ((bf16[32,2,576]{2,1,0:T(2,128)(2,1)}), bf16[32,2,576]{2,1,0:T(2,128)(2,1)S(1)}, u32[]{:S(2)}, u32[]{:S(2)}) async-start(bf16[32,2,576]{2,1,0:T(2,128)(2,1)} %broadcast_in_dim.43), calls=%async_computation.1 | async-start | bytes 163840 | tf_op jit(solution)/shard_map/spread_prefix/all_to_all | solution.py:203
  40.9 3.5 %collective-permute-start = (bf16[16,16,576]{2,1,0:T(8,128)(2,1)S(1)}, bf16[16,16,576]{2,1,0:T(8,128)(2,1)S(1)}, u32[]{:S(2)}, u32[]{:S(2)}) collective-permute-start(bf16[16,16,576]{2,1,0:T(8,128)(2,1)S(1)} %get-tuple-element.15), channel_id=1, source_target_pairs={{0,1},{1,0},{2,3},{3,2},{4,5},{5,4},{6,7},{7,6},{8,9},{9,8},{10,11... | collective-permute-start | bytes 884744 | tf_op jit(solution)/shard_map/sum_heads/ppermute | solution.py:247
  45.3 15.7 %all-to-all-start.2 = ((bf16[16,16,576]{2,1,0:T(8,128)(2,1)}), bf16[16,16,576]{2,1,0:T(8,128)(2,1)S(1)}, u32[]{:S(2)}, u32[]{:S(2)}) async-start(bf16[16,16,576]{2,1,0:T(8,128)(2,1)} %sum_heads.1), calls=%async_computation.2 | async-start | bytes 655360 | tf_op jit(solution)/shard_map/sum_heads/all_to_all | solution.py:257
  61.7 18.3 %all-to-all-start.3 = ((bf16[16,2,576]{2,1,0:T(2,128)(2,1)}), bf16[16,2,576]{2,1,0:T(2,128)(2,1)S(1)}, u32[]{:S(2)}, u32[]{:S(2)}) async-start(bf16[16,2,576]{2,1,0:T(2,128)(2,1)} %broadcast_in_dim.45), calls=%async_computation.3 | async-start | bytes 81920 | tf_op jit(solution)/shard_map/sum_slots/all_to_all | solution.py:276
